TPU v7x, 512 devices: a whole 4x4x16 slice. The times are simulated.
512 devices in a mesh: gx: 16 (over x, z_lo), gy: 8 (over y, core), gz: 4 (over z_hi).
Axes of the slice: x: 4, y: 4, z: 16 (z_hi: 4, z_lo: 4; z = z_hi * 4 + z_lo), core: 2. Of those that a mesh axis runs over, the one named last changes fastest.
Arguments:
- velocity: float32 [3, 256, 256, 512], P(None, 'gx', 'gy', 'gz'), may hold values from -6 to 6
- nut_field: float32 [256, 256, 512], P('gx', 'gy', 'gz'), may hold values from 0.03 to 0.1
- bar_velocity: float32 [3, 256, 256, 512], P(None, 'gx', 'gy', 'gz'), may hold values from -0.3125 to 0.3125
- bar_nut: float32 [256, 256, 512], P('gx', 'gy', 'gz'), may hold values from -6 to 6
- wall_bin: int32 [256, 256, 512], P('gx', 'gy', 'gz'), may hold values from 0 to 31
- fluid_mask: int32 [256, 256, 512], P('gx', 'gy', 'gz'), may hold values 0 or 1
- dist_table: float32 [32], replicated, may hold values from 0.05 to 4
Outputs:
- bar_velocity_in: float32 [3, 256, 256, 512], P(None, 'gx', 'gy', 'gz')
- bar_nut_in: float32 [256, 256, 512], P('gx', 'gy', 'gz')
All inputs are finite; a program needn't handle non-finite values. No bound on the sum of `fluid_mask` on one device may be relied on, other than what follows from the above.
Results may differ from a plain program's by a relative error of at most 0.0003.
Values sent between devices are 32-bit elements; how exact they have to be, the bound alone decides.
A program may use at most 128 MiB of HBM per device.

v0:
```python
import jax
import jax.numpy as jnp
from jax import lax
from jax.sharding import PartitionSpec as P

des_length = 0.65
step_size = 0.25
kappa_sq = 0.1681
coef_prod = 0.1355
coef_dest = 3.239


def extended_2(cells, sides, width):
    for axis, dim in sides:
        count = lax.axis_size(axis)
        ends = count - 1
        head = lax.slice_in_dim(cells, 0, width, axis=dim)
        tail = lax.slice_in_dim(cells, cells.shape[dim] - width, cells.shape[dim], axis=dim)
        cells = jnp.concatenate(
            [
                lax.ppermute(tail, axis, [(i, (i + 1) % count) for i in range(ends)]),
                cells,
                lax.ppermute(head, axis, [((i + 1) % count, i) for i in range(ends)]),
            ],
            axis=dim,
        )
    return cells


def gradient(padded):
    along_x = (padded[:, 2:, 1:-1, 1:-1] - padded[:, :-2, 1:-1, 1:-1]) * 0.5
    along_y = (padded[:, 1:-1, 2:, 1:-1] - padded[:, 1:-1, :-2, 1:-1]) * 0.5
    along_z = (padded[:, 1:-1, 1:-1, 2:] - padded[:, 1:-1, 1:-1, :-2]) * 0.5
    return jnp.stack([along_x, along_y, along_z], 1)


def transpose_grad(extended):
    part_x = (extended[:, 0, :-2, 1:-1, 1:-1] - extended[:, 0, 2:, 1:-1, 1:-1]) * 0.5
    part_y = (extended[:, 1, 1:-1, :-2, 1:-1] - extended[:, 1, 1:-1, 2:, 1:-1]) * 0.5
    part_z = (extended[:, 2, 1:-1, 1:-1, :-2] - extended[:, 2, 1:-1, 1:-1, 2:]) * 0.5
    return part_x + part_y + part_z


def local_section(fields, grads, inv_dist, mask):
    vel = fields[:3]
    nut = fields[3]
    tensor = grads[:3]
    spin = 0.5 * (tensor - jnp.swapaxes(tensor, 0, 1))
    omega = jnp.sqrt(1.0 + 2.0 * jnp.sum(spin * spin, axis=(0, 1)))
    convect = jnp.sum(tensor * vel[None], axis=1)
    new_vel = vel - step_size * mask * convect
    stilde = omega + nut * inv_dist * inv_dist / kappa_sq
    produce = coef_prod * stilde * nut
    destroy = coef_dest * (nut * inv_dist) ** 2
    advect = jnp.sum(vel * grads[3], axis=0)
    new_nut = nut + step_size * mask * (produce - destroy - advect)
    return jnp.concatenate([new_vel, new_nut[None]], 0)


def section_adjoint(fields, grads, inv_dist, mask, bar_out):
    unused, pull = jax.vjp(
        lambda first, second: local_section(first, second, inv_dist, mask), fields, grads
    )
    return pull(bar_out)


def inverse_distance(bins, dist_table):
    bin_ids = jnp.arange(dist_table.shape[0], dtype=jnp.int32)
    looked = jnp.sum(
        jnp.where(bins[None] == bin_ids[:, None, None, None], dist_table[:, None, None, None], 0.0),
        0,
    )
    return 1.0 / jnp.minimum(looked, des_length)


def shards(velocity, nut_field, bar_velocity, bar_nut, wall_bin, fluid_mask, dist_table):
    fields = jnp.concatenate([velocity, nut_field[None]], 0)
    bars = jnp.concatenate([bar_velocity, bar_nut[None]], 0)
    inv_dist = inverse_distance(wall_bin, dist_table)
    mask = fluid_mask.astype(jnp.float32)
    padded = extended_2(fields, (("gx", 1), ("gy", 2), ("gz", 3)), 1)
    grads = gradient(padded)
    bar_local, bar_grads = section_adjoint(fields, grads, inv_dist, mask, bars)
    count_x, count_y, count_z = (fields.shape[1], fields.shape[2], fields.shape[3])
    flat = bar_grads.reshape(12, count_x, count_y, count_z)
    extended = extended_2(flat, (("gx", 1), ("gy", 2), ("gz", 3)), 1)
    extended = extended.reshape(4, 3, count_x + 2, count_y + 2, count_z + 2)
    result = bar_local + transpose_grad(extended)
    return (result[:3], result[3])


def solution(mesh):
    return jax.shard_map(
        shards,
        mesh=mesh,
        in_specs=(
            P(None, "gx", "gy", "gz"),
            P("gx", "gy", "gz"),
            P(None, "gx", "gy", "gz"),
            P("gx", "gy", "gz"),
            P("gx", "gy", "gz"),
            P("gx", "gy", "gz"),
            P(),
        ),
        out_specs=(P(None, "gx", "gy", "gz"), P("gx", "gy", "gz")),
        check_vma=False,
    )
```

profile of v0, /device:TPU:11, one launch (start us, length us, event | category | flops | bytes accessed | tf_op | source)
XLA Modules:
  0.0 143.3 jit_solution(15854401514761699498)
XLA Ops:
  0.7 1.0 pad_maximum_fusion.31
  1.7 3.5 %collective-permute-start.1 = (f32[4,1,32,128]{3,2,1,0:T(8,128)S(1)}, f32[4,1,32,128]{3,2,1,0:T(8,128)S(1)}, u32[]{:S(2)}, u32[]{:S(2)}) collective-permute-start(f32[4,1,32,128]{3,2,1,0:T(8,128)S(1)} %get-tuple-element.18), channel_id=1, source_target_pairs={{0,32},{32,64},{64,96},{96,128},{128,160},{160,192},{192,224},{224... | collective-permute-start | bytes 196616 | tf_op jit(solution)/shard_map/ppermute | solution.py:21
  5.2 4.6 %collective-permute-start = (f32[4,1,32,128]{3,2,1,0:T(8,128)S(1)}, f32[4,1,32,128]{3,2,1,0:T(8,128)S(1)}, u32[]{:S(2)}, u32[]{:S(2)}) collective-permute-start(f32[4,1,32,128]{3,2,1,0:T(8,128)S(1)} %get-tuple-element.19), channel_id=1, source_target_pairs={{32,0},{64,32},{96,64},{128,96},{160,128},{192,160},{224,192},{256... | collective-permute-start | bytes 196616 | tf_op jit(solution)/shard_map/ppermute | solution.py:23
  9.8 1.9 %select_reduce_fusion = f32[16,32,128]{2,1,0:T(8,128)S(1)} fusion(f32[32]{0:T(128)} %param.13, s32[16,32,128]{2,1,0:T(8,128)} %param.11), kind=kLoop, calls=%fused_computation.1 | loop fusion | flops 6225920 | bytes 524416 | tf_op jit(solution)/shard_map/reduce_sum | solution.py:69
  11.7 1.0 convert_multiply_fusion
  12.7 1.2 pad_maximum_fusion.33
  13.9 4.2 %collective-permute-start.3 = (f32[4,18,1,128]{3,2,1,0:T(1,128)S(1)}, f32[4,18,1,128]{3,2,1,0:T(1,128)S(1)}, u32[]{:S(2)}, u32[]{:S(2)}) collective-permute-start(f32[4,18,1,128]{3,2,1,0:T(1,128)S(1)} %get-tuple-element.14), channel_id=1, source_target_pairs={{0,4},{4,8},{8,12},{12,16},{16,20},{20,24},{24,28},{1,5},{5,9},{9,... | collective-permute-start | bytes 110600 | tf_op jit(solution)/shard_map/ppermute | solution.py:21
  18.0 1.9 %collective-permute-start.2 = (f32[4,18,1,128]{3,2,1,0:T(1,128)S(1)}, f32[4,18,1,128]{3,2,1,0:T(1,128)S(1)}, u32[]{:S(2)}, u32[]{:S(2)}) collective-permute-start(f32[4,18,1,128]{3,2,1,0:T(1,128)S(1)} %get-tuple-element.15), channel_id=1, source_target_pairs={{4,0},{8,4},{12,8},{16,12},{20,16},{24,20},{28,24},{5,1},{9,5},{13... | collective-permute-start | bytes 110600 | tf_op jit(solution)/shard_map/ppermute | solution.py:23
  20.0 1.0 negate_multiply_fusion
  21.0 2.3 %collective-permute-done.2 = f32[4,18,1,128]{3,2,1,0:T(1,128)S(1)} collective-permute-done((f32[4,18,1,128]{3,2,1,0:T(1,128)S(1)}, f32[4,18,1,128]{3,2,1,0:T(1,128)S(1)}, u32[]{:S(2)}, u32[]{:S(2)}) %collective-permute-start.2) | collective-permute-done | bytes 36896 | tf_op jit(solution)/shard_map/ppermute | solution.py:23
  23.3 0.6 copy-done.11
  24.2 1.6 %fusion.24 = (f32[4,18,34,1]{3,2,1,0:T(8,128)}, f32[4,18,34,1]{3,2,1,0:T(8,128)S(1)}) fusion(f32[4,18,34,128]{3,2,1,0:T(8,128)S(1)} %pad_maximum_fusion.3), kind=kLoop, calls=%fused_computation.85 | loop fusion | bytes 39168 | tf_op jit(solution)/shard_map/slice | solution.py:17
  25.8 2.6 %copy.29 = f32[4,18,34,1]{2,0,3,1:T(4,128)} copy(f32[4,18,34,1]{3,2,1,0:T(8,128)} %get-tuple-element.10) | data formatting | bytes 19584 | tf_op jit(solution)/shard_map/slice | solution.py:17
  28.4 1.2 copy.31
  29.6 9.4 %collective-permute-start.5 = (f32[4,18,34,1]{2,0,3,1:T(4,128)}, f32[4,18,34,1]{2,0,3,1:T(4,128)}, u32[]{:S(2)}, u32[]{:S(2)}) collective-permute-start(f32[4,18,34,1]{2,0,3,1:T(4,128)} %copy.31), channel_id=1, source_target_pairs={{0,1},{1,2},{2,3},{4,5},{5,6},{6,7},{8,9},{9,10},{10,11},{12,13},{... | collective-permute-start | bytes 29384 | tf_op jit(solution)/shard_map/ppermute | solution.py:21
  39.0 1.3 collective-permute-start.4
  40.3 1.2 fusion.16
  41.4 8.1 %collective-permute-done.4 = f32[4,18,34,1]{2,0,3,1:T(4,128)} collective-permute-done((f32[4,18,34,1]{2,0,3,1:T(4,128)}, f32[4,18,34,1]{2,0,3,1:T(4,128)}, u32[]{:S(2)}, u32[]{:S(2)}) %collective-permute-start.4) | collective-permute-done | bytes 9824 | tf_op jit(solution)/shard_map/ppermute | solution.py:23
  49.5 2.5 %copy.30 = f32[4,18,34,1]{3,2,1,0:T(8,128)} copy(f32[4,18,34,1]{2,0,3,1:T(4,128)} %collective-permute-done.4) | data formatting | bytes 19584 | tf_op jit(solution)/shard_map/ppermute | solution.py:23
  52.1 2.5 %copy.32 = f32[4,18,34,1]{3,2,1,0:T(8,128)} copy(f32[4,18,34,1]{2,0,3,1:T(4,128)} %collective-permute-done.5) | data formatting | bytes 19584 | tf_op jit(solution)/shard_map/ppermute | solution.py:21
  54.6 2.8 %fusion.10 = f32[4,1,16,32,128]{4,3,2,1,0:T(8,128)S(1)} fusion(f32[4,18,34,1]{3,2,1,0:T(8,128)} %copy.32, f32[4,18,1,128]{3,2,1,0:T(1,128)} %copy-done.11, f32[4,18,1,128]{3,2,1,0:T(1,128)} %copy-done.10, f32[4,1,32,128]{3,2,1,0:T(8,128)S(1)} %collective-permute-done, f32[4,1,32,128]{3,2,1,0:T(8,128)S(1)} %collective-permute-done.1, ...), kind=kLoop, calls=%fused_computation.30 | loop fusion | flops 3670016 | bytes 2321536 | tf_op jit(solution)/shard_map/stack | solution.py:34
  57.7 0.8 copy-done.2
  58.5 0.4 multiply_reduce_fusion
  59.5 1.0 fusion.21
  60.9 0.5 bitcast_add_fusion
  61.4 0.6 copy-done.4
  62.0 1.3 fusion.19
  63.3 0.6 pad_add_fusion
  63.9 1.9 %collective-permute-start.6 = (f32[12,1,32,128]{3,2,1,0:T(8,128)S(1)}, f32[12,1,32,128]{3,2,1,0:T(8,128)S(1)}, u32[]{:S(2)}, u32[]{:S(2)}) collective-permute-start(f32[12,1,32,128]{3,2,1,0:T(8,128)S(1)} %get-tuple-element.8), channel_id=1, source_target_pairs={{0,32},{32,64},{64,96},{96,128},{128,160},{160,192},{192,224},{224... | collective-permute-start | bytes 589832 | tf_op jit(solution)/shard_map/ppermute | solution.py:21
  65.8 7.1 %collective-permute-start.7 = (f32[12,1,32,128]{3,2,1,0:T(8,128)S(1)}, f32[12,1,32,128]{3,2,1,0:T(8,128)S(1)}, u32[]{:S(2)}, u32[]{:S(2)}) collective-permute-start(f32[12,1,32,128]{3,2,1,0:T(8,128)S(1)} %get-tuple-element.9), channel_id=1, source_target_pairs={{32,0},{64,32},{96,64},{128,96},{160,128},{192,160},{224,192},{256... | collective-permute-start | bytes 589832 | tf_op jit(solution)/shard_map/ppermute | solution.py:23
  72.9 3.0 %collective-permute-done.6 = f32[12,1,32,128]{3,2,1,0:T(8,128)S(1)} collective-permute-done((f32[12,1,32,128]{3,2,1,0:T(8,128)S(1)}, f32[12,1,32,128]{3,2,1,0:T(8,128)S(1)}, u32[]{:S(2)}, u32[]{:S(2)}) %collective-permute-start.6) | collective-permute-done | bytes 196640 | tf_op jit(solution)/shard_map/ppermute | solution.py:21
  76.0 2.6 %collective-permute-done.7 = f32[12,1,32,128]{3,2,1,0:T(8,128)S(1)} collective-permute-done((f32[12,1,32,128]{3,2,1,0:T(8,128)S(1)}, f32[12,1,32,128]{3,2,1,0:T(8,128)S(1)}, u32[]{:S(2)}, u32[]{:S(2)}) %collective-permute-start.7) | collective-permute-done | bytes 196640 | tf_op jit(solution)/shard_map/ppermute | solution.py:23
  78.7 3.6 %collective-permute-start.8 = (f32[12,18,1,128]{3,2,1,0:T(1,128)S(1)}, f32[12,18,1,128]{3,2,1,0:T(1,128)S(1)}, u32[]{:S(2)}, u32[]{:S(2)}) collective-permute-start(f32[12,18,1,128]{3,2,1,0:T(1,128)S(1)} %get-tuple-element.4), channel_id=1, source_target_pairs={{0,4},{4,8},{8,12},{12,16},{16,20},{20,24},{24,28},{1,5},{5,9},{9,... | collective-permute-start | bytes 331784 | tf_op jit(solution)/shard_map/ppermute | solution.py:21
  82.3 1.9 %collective-permute-start.9 = (f32[12,18,1,128]{3,2,1,0:T(1,128)S(1)}, f32[12,18,1,128]{3,2,1,0:T(1,128)S(1)}, u32[]{:S(2)}, u32[]{:S(2)}) collective-permute-start(f32[12,18,1,128]{3,2,1,0:T(1,128)S(1)} %get-tuple-element.5), channel_id=1, source_target_pairs={{4,0},{8,4},{12,8},{16,12},{20,16},{24,20},{28,24},{5,1},{9,5},{13... | collective-permute-start | bytes 331784 | tf_op jit(solution)/shard_map/ppermute | solution.py:23
  84.2 4.1 %collective-permute-done.9 = f32[12,18,1,128]{3,2,1,0:T(1,128)S(1)} collective-permute-done((f32[12,18,1,128]{3,2,1,0:T(1,128)S(1)}, f32[12,18,1,128]{3,2,1,0:T(1,128)S(1)}, u32[]{:S(2)}, u32[]{:S(2)}) %collective-permute-start.9) | collective-permute-done | bytes 110624 | tf_op jit(solution)/shard_map/ppermute | solution.py:23
  88.4 0.7 pad_maximum_fusion.1
  89.1 4.8 %fusion.22 = (f32[12,18,34,1]{3,2,1,0:T(8,128)}, f32[12,18,34,1]{3,2,1,0:T(8,128)}) fusion(f32[12,18,34,128]{3,2,1,0:T(8,128)S(1)} %pad_maximum_fusion.1), kind=kLoop, calls=%fused_computation.83 | loop fusion | bytes 117504 | tf_op jit(solution)/shard_map/slice | solution.py:18
  94.0 3.9 %copy.37 = f32[12,18,34,1]{2,3,1,0:T(1,128)} copy(f32[12,18,34,1]{3,2,1,0:T(8,128)} %get-tuple-element.2) | data formatting | bytes 58752 | tf_op jit(solution)/shard_map/slice | solution.py:18
  97.9 7.9 %collective-permute-start.10 = (f32[12,18,34,1]{2,3,1,0:T(1,128)}, f32[12,18,34,1]{2,3,1,0:T(1,128)}, u32[]{:S(2)}, u32[]{:S(2)}) collective-permute-start(f32[12,18,34,1]{2,3,1,0:T(1,128)} %copy.37), channel_id=1, source_target_pairs={{0,1},{1,2},{2,3},{4,5},{5,6},{6,7},{8,9},{9,10},{10,11},{12,13},{... | collective-permute-start | bytes 88136 | tf_op jit(solution)/shard_map/ppermute | solution.py:21
  105.8 3.9 %copy.38 = f32[12,18,34,1]{2,3,1,0:T(1,128)} copy(f32[12,18,34,1]{3,2,1,0:T(8,128)} %get-tuple-element.3) | data formatting | bytes 58752 | tf_op jit(solution)/shard_map/slice | solution.py:17
  109.7 1.5 %collective-permute-start.11 = (f32[12,18,34,1]{2,3,1,0:T(1,128)}, f32[12,18,34,1]{2,3,1,0:T(1,128)}, u32[]{:S(2)}, u32[]{:S(2)}) collective-permute-start(f32[12,18,34,1]{2,3,1,0:T(1,128)} %copy.38), channel_id=1, source_target_pairs={{1,0},{2,1},{3,2},{5,4},{6,5},{7,6},{9,8},{10,9},{11,10},{13,12},{... | collective-permute-start | bytes 88136 | tf_op jit(solution)/shard_map/ppermute | solution.py:23
  111.2 3.9 %copy.39 = f32[12,18,34,1]{3,2,1,0:T(8,128)} copy(f32[12,18,34,1]{2,3,1,0:T(1,128)} %collective-permute-done.10) | data formatting | bytes 58752 | tf_op jit(solution)/shard_map/ppermute | solution.py:21
  115.1 11.9 %collective-permute-done.11 = f32[12,18,34,1]{2,3,1,0:T(1,128)} collective-permute-done((f32[12,18,34,1]{2,3,1,0:T(1,128)}, f32[12,18,34,1]{2,3,1,0:T(1,128)}, u32[]{:S(2)}, u32[]{:S(2)}) %collective-permute-start.11) | collective-permute-done | bytes 29408 | tf_op jit(solution)/shard_map/ppermute | solution.py:23
  127.0 4.0 %copy.40 = f32[12,18,34,1]{3,2,1,0:T(8,128)} copy(f32[12,18,34,1]{2,3,1,0:T(1,128)} %collective-permute-done.11) | data formatting | bytes 58752 | tf_op jit(solution)/shard_map/ppermute | solution.py:23
  131.0 9.2 %pad_maximum_fusion = f32[12,18,34,130]{3,2,1,0:T(8,128)S(1)} fusion(f32[12,18,34,1]{3,2,1,0:T(8,128)} %copy.40, f32[12,18,1,128]{3,2,1,0:T(1,128)} %copy-done.9, f32[12,1,32,128]{3,2,1,0:T(8,128)S(1)} %collective-permute-done.7, f32[12,16,32,128]{3,2,1,0:T(8,128)S(1)} %bitcast.80, f32[12,1,32,128]{3,2,1,0:T(8,128)S(1)} %collective-permute-done.6, ...), kind=kLoop, calls=%fused_computation | loop fusion | flops 5728320 | bytes 7637760 | tf_op jit(solution)/shard_map/concatenate | solution.py:19
  140.2 1.4 fusion.4
  141.6 0.7 slice_bitcast_fusion.6
  142.3 0.9 slice.131
  (35 shorter events, 1.8 us)
Async XLA Ops:
  0.6 23.3 %copy-start = (f32[3,16,32,128]{3,2,1,0:T(8,128)S(1)}, f32[3,16,32,128]{3,2,1,0:T(8,128)}, u32[]{:S(2)}) copy-start(f32[3,16,32,128]{3,2,1,0:T(8,128)} %param.7) | copy-start | bytes 2359300
  0.6 23.3 %copy-start.1 = (f32[16,32,128]{2,1,0:T(8,128)S(1)}, f32[16,32,128]{2,1,0:T(8,128)}, u32[]{:S(2)}) copy-start(f32[16,32,128]{2,1,0:T(8,128)} %param.8) | copy-start | bytes 786436
  0.7 19.3 %copy-start.3 = (f32[3,16,32,128]{3,2,1,0:T(8,128)S(1)}, f32[3,16,32,128]{3,2,1,0:T(8,128)}, u32[]{:S(2)}) copy-start(f32[3,16,32,128]{3,2,1,0:T(8,128)} %param.9) | copy-start | bytes 2359300
  1.7 11.0 %collective-permute-start.1 = (f32[4,1,32,128]{3,2,1,0:T(8,128)S(1)}, f32[4,1,32,128]{3,2,1,0:T(8,128)S(1)}, u32[]{:S(2)}, u32[]{:S(2)}) collective-permute-start(f32[4,1,32,128]{3,2,1,0:T(8,128)S(1)} %get-tuple-element.18), channel_id=1, source_target_pairs={{0,32},{32,64},{64,96},{96,128},{128,160},{160,192},{192,224},{224... | collective-permute-start | bytes 196616 | tf_op jit(solution)/shard_map/ppermute | solution.py:21
  5.2 7.5 %collective-permute-start = (f32[4,1,32,128]{3,2,1,0:T(8,128)S(1)}, f32[4,1,32,128]{3,2,1,0:T(8,128)S(1)}, u32[]{:S(2)}, u32[]{:S(2)}) collective-permute-start(f32[4,1,32,128]{3,2,1,0:T(8,128)S(1)} %get-tuple-element.19), channel_id=1, source_target_pairs={{32,0},{64,32},{96,64},{128,96},{160,128},{192,160},{224,192},{256... | collective-permute-start | bytes 196616 | tf_op jit(solution)/shard_map/ppermute | solution.py:23
  13.9 7.1 %collective-permute-start.3 = (f32[4,18,1,128]{3,2,1,0:T(1,128)S(1)}, f32[4,18,1,128]{3,2,1,0:T(1,128)S(1)}, u32[]{:S(2)}, u32[]{:S(2)}) collective-permute-start(f32[4,18,1,128]{3,2,1,0:T(1,128)S(1)} %get-tuple-element.14), channel_id=1, source_target_pairs={{0,4},{4,8},{8,12},{12,16},{16,20},{20,24},{24,28},{1,5},{5,9},{9,... | collective-permute-start | bytes 110600 | tf_op jit(solution)/shard_map/ppermute | solution.py:21
  18.0 5.3 %collective-permute-start.2 = (f32[4,18,1,128]{3,2,1,0:T(1,128)S(1)}, f32[4,18,1,128]{3,2,1,0:T(1,128)S(1)}, u32[]{:S(2)}, u32[]{:S(2)}) collective-permute-start(f32[4,18,1,128]{3,2,1,0:T(1,128)S(1)} %get-tuple-element.15), channel_id=1, source_target_pairs={{4,0},{8,4},{12,8},{16,12},{20,16},{24,20},{28,24},{5,1},{9,5},{13... | collective-permute-start | bytes 110600 | tf_op jit(solution)/shard_map/ppermute | solution.py:23
  21.0 2.3 %copy-start.10 = (f32[4,18,1,128]{3,2,1,0:T(1,128)}, f32[4,18,1,128]{3,2,1,0:T(1,128)S(1)}, u32[]{:S(2)}) copy-start(f32[4,18,1,128]{3,2,1,0:T(1,128)S(1)} %collective-permute-done.3) | copy-start | bytes 110596
  23.3 0.6 copy-start.11
  29.6 22.5 %collective-permute-start.5 = (f32[4,18,34,1]{2,0,3,1:T(4,128)}, f32[4,18,34,1]{2,0,3,1:T(4,128)}, u32[]{:S(2)}, u32[]{:S(2)}) collective-permute-start(f32[4,18,34,1]{2,0,3,1:T(4,128)} %copy.31), channel_id=1, source_target_pairs={{0,1},{1,2},{2,3},{4,5},{5,6},{6,7},{8,9},{9,10},{10,11},{12,13},{... | collective-permute-start | bytes 29384 | tf_op jit(solution)/shard_map/ppermute | solution.py:21
  39.0 10.5 %collective-permute-start.4 = (f32[4,18,34,1]{2,0,3,1:T(4,128)}, f32[4,18,34,1]{2,0,3,1:T(4,128)}, u32[]{:S(2)}, u32[]{:S(2)}) collective-permute-start(f32[4,18,34,1]{2,0,3,1:T(4,128)} %copy.29), channel_id=1, source_target_pairs={{1,0},{2,1},{3,2},{5,4},{6,5},{7,6},{9,8},{10,9},{11,10},{13,12},{... | collective-permute-start | bytes 29384 | tf_op jit(solution)/shard_map/ppermute | solution.py:23
  57.3 1.1 copy-start.2
  58.5 0.9 copy-start.7
  58.5 1.0 copy-start.12
  60.9 1.1 copy-start.4
  63.9 12.1 %collective-permute-start.6 = (f32[12,1,32,128]{3,2,1,0:T(8,128)S(1)}, f32[12,1,32,128]{3,2,1,0:T(8,128)S(1)}, u32[]{:S(2)}, u32[]{:S(2)}) collective-permute-start(f32[12,1,32,128]{3,2,1,0:T(8,128)S(1)} %get-tuple-element.8), channel_id=1, source_target_pairs={{0,32},{32,64},{64,96},{96,128},{128,160},{160,192},{192,224},{224... | collective-permute-start | bytes 589832 | tf_op jit(solution)/shard_map/ppermute | solution.py:21
  65.8 12.7 %collective-permute-start.7 = (f32[12,1,32,128]{3,2,1,0:T(8,128)S(1)}, f32[12,1,32,128]{3,2,1,0:T(8,128)S(1)}, u32[]{:S(2)}, u32[]{:S(2)}) collective-permute-start(f32[12,1,32,128]{3,2,1,0:T(8,128)S(1)} %get-tuple-element.9), channel_id=1, source_target_pairs={{32,0},{64,32},{96,64},{128,96},{160,128},{192,160},{224,192},{256... | collective-permute-start | bytes 589832 | tf_op jit(solution)/shard_map/ppermute | solution.py:23
  78.7 5.5 %collective-permute-start.8 = (f32[12,18,1,128]{3,2,1,0:T(1,128)S(1)}, f32[12,18,1,128]{3,2,1,0:T(1,128)S(1)}, u32[]{:S(2)}, u32[]{:S(2)}) collective-permute-start(f32[12,18,1,128]{3,2,1,0:T(1,128)S(1)} %get-tuple-element.4), channel_id=1, source_target_pairs={{0,4},{4,8},{8,12},{12,16},{16,20},{20,24},{24,28},{1,5},{5,9},{9,... | collective-permute-start | bytes 331784 | tf_op jit(solution)/shard_map/ppermute | solution.py:21
  82.3 6.1 %collective-permute-start.9 = (f32[12,18,1,128]{3,2,1,0:T(1,128)S(1)}, f32[12,18,1,128]{3,2,1,0:T(1,128)S(1)}, u32[]{:S(2)}, u32[]{:S(2)}) collective-permute-start(f32[12,18,1,128]{3,2,1,0:T(1,128)S(1)} %get-tuple-element.5), channel_id=1, source_target_pairs={{4,0},{8,4},{12,8},{16,12},{20,16},{24,20},{28,24},{5,1},{9,5},{13... | collective-permute-start | bytes 331784 | tf_op jit(solution)/shard_map/ppermute | solution.py:23
  84.2 4.9 %copy-start.8 = (f32[12,18,1,128]{3,2,1,0:T(1,128)}, f32[12,18,1,128]{3,2,1,0:T(1,128)S(1)}, u32[]{:S(2)}) copy-start(f32[12,18,1,128]{3,2,1,0:T(1,128)S(1)} %collective-permute-done.8) | copy-start | bytes 331780
  88.4 0.7 copy-start.9
  97.9 13.3 %collective-permute-start.10 = (f32[12,18,34,1]{2,3,1,0:T(1,128)}, f32[12,18,34,1]{2,3,1,0:T(1,128)}, u32[]{:S(2)}, u32[]{:S(2)}) collective-permute-start(f32[12,18,34,1]{2,3,1,0:T(1,128)} %copy.37), channel_id=1, source_target_pairs={{0,1},{1,2},{2,3},{4,5},{5,6},{6,7},{8,9},{9,10},{10,11},{12,13},{... | collective-permute-start | bytes 88136 | tf_op jit(solution)/shard_map/ppermute | solution.py:21
  109.7 17.3 %collective-permute-start.11 = (f32[12,18,34,1]{2,3,1,0:T(1,128)}, f32[12,18,34,1]{2,3,1,0:T(1,128)}, u32[]{:S(2)}, u32[]{:S(2)}) collective-permute-start(f32[12,18,34,1]{2,3,1,0:T(1,128)} %copy.38), channel_id=1, source_target_pairs={{1,0},{2,1},{3,2},{5,4},{6,5},{7,6},{9,8},{10,9},{11,10},{13,12},{... | collective-permute-start | bytes 88136 | tf_op jit(solution)/shard_map/ppermute | solution.py:23
  131.0 9.2 %copy-start.5 = (f32[3,16,32,128]{3,2,1,0:T(8,128)S(1)}, f32[3,16,32,128]{3,2,1,0:T(8,128)}, u32[]{:S(2)}) copy-start(f32[3,16,32,128]{3,2,1,0:T(8,128)} %get-tuple-element.21) | copy-start | bytes 2359300
  131.0 9.2 %copy-start.6 = (f32[1,16,32,128]{3,2,1,0:T(8,128)S(1)}, f32[1,16,32,128]{3,2,1,0:T(8,128)}, u32[]{:S(2)}) copy-start(f32[1,16,32,128]{3,2,1,0:T(8,128)} %get-tuple-element.16) | copy-start | bytes 786436
where the time goes:
time: 144 us; the launch traced here: 143 us
  starting transfers between devices  48.8 us (34%)
  local copies, waits for them, and re-layouts  35 us (24%)
  waiting for transfers between devices  32 us (22%)
  other arithmetic  26.5 us (18%)
    ppermute x6, starting transfers between devices, extended_2(): lax.ppermute(tail, axis, [(i, (i + 1) % count) for i in range(ends)])  30.5 us
    ppermute x6, waiting for transfers between devices, extended_2(): lax.ppermute(head, axis, [((i + 1) % count, i) for i in range(ends)])  29 us
    ppermute x6, starting transfers between devices, extended_2(): lax.ppermute(head, axis, [((i + 1) % count, i) for i in range(ends)])  18.3 us
    concatenate x4, other arithmetic, extended_2(): jnp.concatenate([lax.ppermute(tail, axis, [(i, (i + 1) % count) for i in...  11.3 us
    slice x4, local copies, waits for them, and re-layouts, extended_2(): lax.slice_in_dim(cells, cells.shape[dim] - width, cells.shape[dim], axis=...  10 us
    slice x3, local copies, waits for them, and re-layouts, extended_2(): head = lax.slice_in_dim(cells, 0, width, axis=dim)  8.14 us
    ppermute x2, local copies, waits for them, and re-layouts, extended_2(): lax.ppermute(head, axis, [((i + 1) % count, i) for i in range(ends)])  6.51 us
    ppermute x2, local copies, waits for them, and re-layouts, extended_2(): lax.ppermute(tail, axis, [(i, (i + 1) % count) for i in range(ends)])  6.43 us
  transfers between devices with their start and end apart: 12, of which 6 were waited for; matrix products, arithmetic and copies ran while one was open for 11% of the time, Pallas kernels for 0%

commit v1 on v0

v1 whole, which is shorter than its diff:
```python
import functools

import jax
import jax.numpy as jnp
from jax import lax
from jax.experimental import pallas as pl
from jax.experimental.pallas import tpu as pltpu
from jax.sharding import PartitionSpec as P

des_length = 0.65
step_size = 0.25
kappa_sq = 0.1681
coef_prod = 0.1355
coef_dest = 3.239

MESH = pl.DeviceIdType.MESH
AXES = ("gx", "gy", "gz")
PAD = 8
LANES = 128


def section_kernel(
    counts, vel, nut, bvel, bnut, bins, mask, dist, ovel, onut,
    q, bar, bin_v, mask_v, nx, ny, res, comb, edge_t, y_halo, z_send, z_recv,
    w_send, w_recv, load_sem, store_sem, send_sem, recv_sem,
):
    cx, cy = nut.shape[0], nut.shape[1]
    tiles = cy // 8
    group = LANES // cy
    groups = cx // group
    rows = pl.ds(PAD, cy)
    planes = pl.ds(1, cx)
    f32 = jnp.float32

    pos = [lax.axis_index(a) for a in AXES]
    has = [(pos[d] > 0, pos[d] < counts[d] - 1) for d in range(3)]
    peer = [({AXES[d]: pos[d] - 1}, {AXES[d]: pos[d] + 1}) for d in range(3)]

    barrier = pltpu.get_barrier_semaphore()
    for d in range(3):
        for s in range(2):
            @pl.when(has[d][s])
            def _():
                pl.semaphore_signal(barrier, inc=1, device_id=peer[d][s], device_id_type=MESH)

    loads = [
        pltpu.make_async_copy(vel, q.at[0:3, planes, rows, :], load_sem.at[0]),
        pltpu.make_async_copy(nut, q.at[3, planes, rows, :], load_sem.at[1]),
        pltpu.make_async_copy(bvel, bar.at[0:3], load_sem.at[2]),
        pltpu.make_async_copy(bnut, bar.at[3], load_sem.at[3]),
        pltpu.make_async_copy(mask, mask_v, load_sem.at[4]),
        pltpu.make_async_copy(bins, bin_v, load_sem.at[5]),
    ]
    for copy in loads:
        copy.start()

    def remote(src, dst, slot, d, s):
        return pltpu.make_async_remote_copy(
            src_ref=src, dst_ref=dst, send_sem=send_sem.at[slot], recv_sem=recv_sem.at[slot],
            device_id=peer[d][s], device_id_type=MESH,
        )

    first = [[None, None] for _ in range(3)]
    for s in range(2):
        end = (0, cx - 1)[s]
        halo = (cx + 1, 0)[s]
        first[0][s] = [
            remote(vel.at[:, end], q.at[0:3, halo, rows, :], 0 + s, 0, s),
            remote(nut.at[end], q.at[3, halo, rows, :], 2 + s, 0, s),
        ]
        end = (0, cy - 1)[s]
        halo = (PAD + cy, PAD - 1)[s]
        first[1][s] = [
            remote(vel.at[:, :, end, :], q.at[0:3, planes, halo, :], 4 + s, 1, s),
            remote(nut.at[:, end, :], q.at[3, planes, halo, :], 6 + s, 1, s),
        ]
        first[2][s] = [remote(z_send.at[s], z_recv.at[1 - s], 8 + s, 2, s)]
    second = [[None, None] for _ in range(3)]
    for s in range(2):
        end = (1, cx)[s]
        halo = (cx + 1, 0)[s]
        second[0][s] = [remote(nx.at[:, end], nx.at[:, halo], 10 + s, 0, s)]
        end = (PAD, PAD + cy - 1)[s]
        second[1][s] = [remote(ny.at[:, :, end, :], y_halo.at[1 - s], 12 + s, 1, s)]
        second[2][s] = [remote(w_send.at[s], w_recv.at[1 - s], 14 + s, 2, s)]

    def start(copies, d):
        for s in range(2):
            @pl.when(has[d][s])
            def _():
                for copy in copies[d][s]:
                    copy.start()

    def arrive(copies, d):
        for s in range(2):
            @pl.when(has[d][1 - s])
            def _():
                for copy in copies[d][s]:
                    copy.wait_recv()

    def sent(copies, d):
        for s in range(2):
            @pl.when(has[d][s])
            def _():
                for copy in copies[d][s]:
                    copy.wait_send()

    for s in range(2):
        @pl.when(jnp.logical_not(has[0][s]))
        def _():
            halo = (0, cx + 1)[s]
            q[:, halo, rows, :] = jnp.zeros((4, cy, LANES), f32)
            nx[:, halo] = jnp.zeros((4, cy, LANES), f32)

        @pl.when(jnp.logical_not(has[1][s]))
        def _():
            halo = (PAD - 1, PAD + cy)[s]
            for f in range(4):
                q[f, planes, halo, :] = jnp.zeros((cx, LANES), f32)
            y_halo[s] = jnp.zeros((4, cx, LANES), f32)

        @pl.when(jnp.logical_not(has[2][s]))
        def _():
            z_recv[s] = jnp.zeros((4 * groups, LANES), f32)
            w_recv[s] = jnp.zeros((4 * groups, LANES), f32)

    present = sum(h.astype(jnp.int32) for pair in has for h in pair)
    pl.semaphore_wait(barrier, present)
    start(first, 0)
    start(first, 1)

    lane = lax.broadcasted_iota(jnp.int32, (8, LANES), 1)
    low = lane == 0
    high = lane == LANES - 1
    pairs = [lane < 2 * f + 2 for f in range(3)]

    def merge(parts):
        rolled = [pltpu.roll(part, 2 * f + 1, 1) for f, part in enumerate(parts)]
        out = rolled[3]
        for f in (2, 1, 0):
            out = jnp.where(pairs[f], rolled[f], out)
        return out

    def pack(dst):
        for g in range(groups):
            turned = comb[g * group:(g + 1) * group].reshape(LANES, LANES).T
            for f in range(4):
                dst[1, f * groups + g:f * groups + g + 1, :] = turned[2 * f:2 * f + 1]
                dst[0, f * groups + g:f * groups + g + 1, :] = turned[2 * f + 1:2 * f + 2]

    def unpack(src, sign):
        for g in range(groups):
            parts = []
            for f in range(4):
                parts.append(src[0, f * groups + g:f * groups + g + 1, :] * sign)
                parts.append(src[1, f * groups + g:f * groups + g + 1, :])
            parts.append(jnp.zeros((LANES - 8, LANES), f32))
            turned = jnp.concatenate(parts, axis=0).T
            edge_t[g * group:(g + 1) * group] = turned.reshape(group, cy, LANES)

    def halo_lanes(edges, f):
        return pltpu.roll(edges, LANES - (2 * f + 1), 1)

    loads[0].wait()
    loads[1].wait()

    def pack_plane(p, carry):
        for t in range(tiles):
            comb[p, 8 * t:8 * t + 8, :] = merge(
                [q[f, p + 1, PAD + 8 * t:PAD + 8 * t + 8, :] for f in range(4)]
            )
        return carry

    lax.fori_loop(0, cx, pack_plane, 0)
    pack(z_send)
    start(first, 2)

    for copy in loads[2:]:
        copy.wait()
    table = 1.0 / jnp.minimum(dist[...], des_length)
    table = table * table * (2.0 * (2.0 * coef_prod / kappa_sq - 2.0 * coef_dest))
    table = jnp.broadcast_to(
        jnp.pad(table, (0, LANES - table.shape[0])).reshape(1, LANES), (8, LANES)
    )

    for d in range(3):
        arrive(first, d)
    unpack(z_recv, 1.0)

    half = 0.5 * step_size

    def plane(p, carry):
        for t in range(tiles):
            lo = 8 * t
            mid = slice(PAD + lo, PAD + lo + 8)
            up = slice(PAD + lo + 1, PAD + lo + 9)
            down = slice(PAD + lo - 1, PAD + lo + 7)
            here = slice(lo, lo + 8)
            edges = edge_t[p, here, :]
            cell = [q[f, p + 1, mid, :] for f in range(4)]
            diff = []
            for f in range(4):
                ends = halo_lanes(edges, f)
                along_z = pltpu.roll(jnp.where(low, ends, cell[f]), LANES - 1, 1) - pltpu.roll(
                    jnp.where(high, ends, cell[f]), 1, 1
                )
                diff.append([
                    q[f, p + 2, mid, :] - q[f, p, mid, :],
                    q[f, p + 1, up, :] - q[f, p + 1, down, :],
                    along_z,
                ])
            wet = jnp.where(mask_v[p, here, :] != 0, half, 0.0)
            bars = [bar[i, p, here, :] for i in range(4)]
            scaled = [wet * b for b in bars]
            spin = {
                (0, 1): diff[0][1] - diff[1][0],
                (0, 2): diff[0][2] - diff[2][0],
                (1, 2): diff[1][2] - diff[2][1],
            }
            total = 1.0 + 0.25 * (
                spin[0, 1] * spin[0, 1] + spin[0, 2] * spin[0, 2] + spin[1, 2] * spin[1, 2]
            )
            inverse = lax.rsqrt(total)
            omega = total * inverse
            weight = scaled[3] * cell[3] * inverse * (0.5 * coef_prod)
            turn = {key: weight * value for key, value in spin.items()}
            flux = [[scaled[i] * cell[j] for j in range(3)] for i in range(4)]
            for (i, j), value in turn.items():
                flux[i][j] = flux[i][j] - value
                flux[j][i] = flux[j][i] + value
            for i in range(4):
                nx[i, p + 1, here, :] = flux[i][0]
                ny[i, p, mid, :] = flux[i][1]
            comb[p, here, :] = merge([flux[i][2] for i in range(4)])
            near = jnp.take_along_axis(table, bin_v[p, here, :], axis=1)
            for j in range(4):
                value = bars[j]
                if j < 3:
                    for i in range(4):
                        value = value - scaled[i] * diff[i][j]
                else:
                    value = value + scaled[3] * ((2.0 * coef_prod) * omega + cell[3] * near)
                value = value + (
                    pltpu.roll(jnp.where(low, 0.0, flux[j][2]), LANES - 1, 1)
                    - pltpu.roll(jnp.where(high, 0.0, flux[j][2]), 1, 1)
                )
                res[j, p, here, :] = value
        return carry

    plane(0, 0)
    plane(cx - 1, 0)
    start(second, 0)
    lax.fori_loop(1, cx - 1, plane, 0)
    start(second, 1)
    pack(w_send)
    start(second, 2)

    for i in range(4):
        ny[i, :, PAD - 1, :] = jnp.zeros((cx, LANES), f32)
        ny[i, :, PAD + cy, :] = jnp.zeros((cx, LANES), f32)

    def finish(p, carry):
        for t in range(tiles):
            lo = 8 * t
            here = slice(lo, lo + 8)
            up = slice(PAD + lo + 1, PAD + lo + 9)
            down = slice(PAD + lo - 1, PAD + lo + 7)
            for i in range(4):
                res[i, p, here, :] = res[i, p, here, :] + (
                    (nx[i, p + 2, here, :] - nx[i, p, here, :])
                    + (ny[i, p, up, :] - ny[i, p, down, :])
                )
        return carry

    lax.fori_loop(1, cx - 1, finish, 0)
    arrive(second, 0)
    finish(0, 0)
    finish(cx - 1, 0)
    arrive(second, 1)
    for i in range(4):
        res[i, :, 0, :] = res[i, :, 0, :] - y_halo[0, i]
        res[i, :, cy - 1, :] = res[i, :, cy - 1, :] + y_halo[1, i]
    arrive(second, 2)
    unpack(w_recv, -1.0)
    outer = jnp.logical_or(low, high)

    def sides(p, carry):
        for t in range(tiles):
            here = slice(8 * t, 8 * t + 8)
            edges = edge_t[p, here, :]
            for i in range(4):
                ends = pltpu.roll(edges, (LANES - 2 * i) % LANES, 1)
                ends = jnp.where(low, ends, pltpu.roll(edges, LANES - 2 - 2 * i, 1))
                res[i, p, here, :] = res[i, p, here, :] + jnp.where(outer, ends, 0.0)
        return carry

    lax.fori_loop(0, cx, sides, 0)
    stores = [
        pltpu.make_async_copy(res.at[0:3], ovel, store_sem.at[0]),
        pltpu.make_async_copy(res.at[3], onut, store_sem.at[1]),
    ]
    for copy in stores:
        copy.start()
    for d in range(3):
        sent(first, d)
        sent(second, d)
    for copy in stores:
        copy.wait()


def shards(counts, *args):
    velocity, nut_field = args[0], args[1]
    cx, cy, cz = nut_field.shape
    f32 = jnp.float32
    group = LANES // cy
    packed = (2, 4 * (cx // group), LANES)
    any_spec = pl.BlockSpec(memory_space=pl.ANY)
    return pl.pallas_call(
        functools.partial(section_kernel, counts),
        out_shape=(
            jax.ShapeDtypeStruct(velocity.shape, f32),
            jax.ShapeDtypeStruct(nut_field.shape, f32),
        ),
        in_specs=[any_spec] * 6 + [pl.BlockSpec(memory_space=pltpu.VMEM)],
        out_specs=(any_spec, any_spec),
        scratch_shapes=[
            pltpu.VMEM((4, cx + 2, cy + 2 * PAD, cz), f32),
            pltpu.VMEM((4, cx, cy, cz), f32),
            pltpu.VMEM((cx, cy, cz), jnp.int32),
            pltpu.VMEM((cx, cy, cz), jnp.int32),
            pltpu.VMEM((4, cx + 2, cy, cz), f32),
            pltpu.VMEM((4, cx, cy + 2 * PAD, cz), f32),
            pltpu.VMEM((4, cx, cy, cz), f32),
            pltpu.VMEM((cx, cy, cz), f32),
            pltpu.VMEM((cx, cy, cz), f32),
            pltpu.VMEM((2, 4, cx, cz), f32),
            pltpu.VMEM(packed, f32),
            pltpu.VMEM(packed, f32),
            pltpu.VMEM(packed, f32),
            pltpu.VMEM(packed, f32),
            pltpu.SemaphoreType.DMA((6,)),
            pltpu.SemaphoreType.DMA((2,)),
            pltpu.SemaphoreType.DMA((16,)),
            pltpu.SemaphoreType.DMA((16,)),
        ],
        compiler_params=pltpu.CompilerParams(
            collective_id=0, has_side_effects=True, vmem_limit_bytes=32 * 1024 * 1024
        ),
        name="section_adjoint",
    )(*args)


def solution(mesh):
    counts = tuple(mesh.shape[a] for a in AXES)
    field = P("gx", "gy", "gz")
    tensor = P(None, "gx", "gy", "gz")
    return jax.shard_map(
        functools.partial(shards, counts),
        mesh=mesh,
        in_specs=(tensor, field, tensor, field, field, field, P()),
        out_specs=(tensor, field),
        check_vma=False,
    )
```

time: 144 us -> 39.2 us (0.27)
  the two profiles are of different devices: /device:TPU:11 before, /device:TPU:6 now
where the time goes in v1:
time: 39.2 us; the launch traced here: 38.6 us
  Pallas kernels  29.7 us (76%)
  local copies, waits for them, and re-layouts  8.3 us (21%)
  between operations  0.66 us (2%)
    pallas_call x1, Pallas kernels, shards(): pl.pallas_call(functools.partial(section_kernel, counts), out_shape=(jax....  29.7 us
    unnamed x16, local copies, waits for them, and re-layouts  8.3 us

profile of v1, /device:TPU:6, one launch (start us, length us, event | category | flops | bytes accessed | tf_op | source)
XLA Modules:
  0.0 38.6 jit_solution(3160319224178039699)
XLA Ops:
  0.6 0.0 copy-start
  0.6 1.1 %copy-done = f32[3,16,32,128]{3,2,1,0:T(8,128)S(1)} copy-done((f32[3,16,32,128]{3,2,1,0:T(8,128)S(1)}, f32[3,16,32,128]{3,2,1,0:T(8,128)}, u32[]{:S(2)}) %copy-start) | copy-done | bytes 786456
  1.8 0.0 copy-start.1
  1.8 1.1 %copy-done.1 = f32[3,16,32,128]{3,2,1,0:T(8,128)S(1)} copy-done((f32[3,16,32,128]{3,2,1,0:T(8,128)S(1)}, f32[3,16,32,128]{3,2,1,0:T(8,128)}, u32[]{:S(2)}) %copy-start.1) | copy-done | bytes 786456
  2.9 0.0 copy-start.2
  2.9 0.9 %copy-done.2 = f32[16,32,128]{2,1,0:T(8,128)S(1)} copy-done((f32[16,32,128]{2,1,0:T(8,128)S(1)}, f32[16,32,128]{2,1,0:T(8,128)}, u32[]{:S(2)}) %copy-start.2) | copy-done | bytes 262168
  3.9 0.0 copy-start.3
  3.9 0.9 %copy-done.3 = f32[16,32,128]{2,1,0:T(8,128)S(1)} copy-done((f32[16,32,128]{2,1,0:T(8,128)S(1)}, f32[16,32,128]{2,1,0:T(8,128)}, u32[]{:S(2)}) %copy-start.3) | copy-done | bytes 262168
  4.8 0.0 copy-start.4
  4.8 0.9 %copy-done.4 = s32[16,32,128]{2,1,0:T(8,128)S(1)} copy-done((s32[16,32,128]{2,1,0:T(8,128)S(1)}, s32[16,32,128]{2,1,0:T(8,128)}, u32[]{:S(2)}) %copy-start.4) | copy-done | bytes 262168
  5.8 0.0 copy-start.5
  5.8 0.9 %copy-done.5 = s32[16,32,128]{2,1,0:T(8,128)S(1)} copy-done((s32[16,32,128]{2,1,0:T(8,128)S(1)}, s32[16,32,128]{2,1,0:T(8,128)}, u32[]{:S(2)}) %copy-start.5) | copy-done | bytes 262168
  6.7 0.0 copy-start.6
  6.7 0.7 %copy-done.6 = f32[32]{0:T(128)S(1)} copy-done((f32[32]{0:T(128)S(1)}, f32[32]{0:T(128)}, u32[]{:S(2)}) %copy-start.6) | copy-done | bytes 152
  7.4 29.7 %section_adjoint.1 = (f32[3,16,32,128]{3,2,1,0:T(8,128)S(1)}, f32[16,32,128]{2,1,0:T(8,128)S(1)}) custom-call(f32[3,16,32,128]{3,2,1,0:T(8,128)S(1)} %copy-done, f32[16,32,128]{2,1,0:T(8,128)S(1)} %copy-done.2, f32[3,16,32,128]{3,2,1,0:T(8,128)S(1)} %copy-done.1, f32[16,32,128]{2,1,0:T(8,128)S(1)} %copy-done.3, s32[16,32,128]{2,1,0:T(8,128)S(1)} %copy-done.4, ...), custom_call_target="tpu_custom_call" | custom-call | tf_op jit(solution)/shard_map/section_adjoint/pallas_call | solution.py:318
  37.0 0.9 %copy.11 = f32[3,16,32,128]{3,2,1,0:T(8,128)} copy(f32[3,16,32,128]{3,2,1,0:T(8,128)S(1)} %get-tuple-element.4) | data formatting | bytes 1572864
  37.9 0.7 %copy.12 = f32[16,32,128]{2,1,0:T(8,128)} copy(f32[16,32,128]{2,1,0:T(8,128)S(1)} %get-tuple-element.5) | data formatting | bytes 524288
Async XLA Ops:
  0.6 1.1 %copy-start = (f32[3,16,32,128]{3,2,1,0:T(8,128)S(1)}, f32[3,16,32,128]{3,2,1,0:T(8,128)}, u32[]{:S(2)}) copy-start(f32[3,16,32,128]{3,2,1,0:T(8,128)} %vel.1) | copy-start | bytes 2359300
  1.8 1.1 %copy-start.1 = (f32[3,16,32,128]{3,2,1,0:T(8,128)S(1)}, f32[3,16,32,128]{3,2,1,0:T(8,128)}, u32[]{:S(2)}) copy-start(f32[3,16,32,128]{3,2,1,0:T(8,128)} %bvel.1) | copy-start | bytes 2359300
  2.9 0.9 %copy-start.2 = (f32[16,32,128]{2,1,0:T(8,128)S(1)}, f32[16,32,128]{2,1,0:T(8,128)}, u32[]{:S(2)}) copy-start(f32[16,32,128]{2,1,0:T(8,128)} %nut.1) | copy-start | bytes 786436
  3.9 0.9 %copy-start.3 = (f32[16,32,128]{2,1,0:T(8,128)S(1)}, f32[16,32,128]{2,1,0:T(8,128)}, u32[]{:S(2)}) copy-start(f32[16,32,128]{2,1,0:T(8,128)} %bnut.1) | copy-start | bytes 786436
  4.8 0.9 %copy-start.4 = (s32[16,32,128]{2,1,0:T(8,128)S(1)}, s32[16,32,128]{2,1,0:T(8,128)}, u32[]{:S(2)}) copy-start(s32[16,32,128]{2,1,0:T(8,128)} %bins.1) | copy-start | bytes 786436
  5.8 0.9 %copy-start.5 = (s32[16,32,128]{2,1,0:T(8,128)S(1)}, s32[16,32,128]{2,1,0:T(8,128)}, u32[]{:S(2)}) copy-start(s32[16,32,128]{2,1,0:T(8,128)} %mask.1) | copy-start | bytes 786436
  6.7 0.7 %copy-start.6 = (f32[32]{0:T(128)S(1)}, f32[32]{0:T(128)}, u32[]{:S(2)}) copy-start(f32[32]{0:T(128)} %dist.1) | copy-start | bytes 388

commit v2 on v1

v2 whole, which is shorter than its diff:
```python
import functools

import jax
import jax.numpy as jnp
from jax import lax
from jax.experimental import pallas as pl
from jax.experimental.pallas import tpu as pltpu
from jax.sharding import PartitionSpec as P

des_length = 0.65
step_size = 0.25
kappa_sq = 0.1681
coef_prod = 0.1355
coef_dest = 3.239

MESH = pl.DeviceIdType.MESH
AXES = ("gx", "gy", "gz")
PAD = 8
LANES = 128


def section_kernel(
    counts, vel, nut, bvel, bnut, bins, mask, dist, ovel, onut,
    q, bar, bin_v, mask_v, dist_v, near, dz, nx, ny, parts, pick, place, y_halo,
    z_send, z_recv, w_send, w_recv, load_sem, send_sem, recv_sem,
):
    cx, cy = nut.shape[0], nut.shape[1]
    tiles = cy // 8
    group = LANES // cy
    groups = cx // group
    rows = pl.ds(PAD, cy)
    planes = pl.ds(1, cx)
    f32, bf16 = jnp.float32, jnp.bfloat16

    pos = [lax.axis_index(a) for a in AXES]
    has = [(pos[d] > 0, pos[d] < counts[d] - 1) for d in range(3)]
    peer = [({AXES[d]: pos[d] - 1}, {AXES[d]: pos[d] + 1}) for d in range(3)]

    loads = [
        pltpu.make_async_copy(vel, q.at[0:3, planes, rows, :], load_sem.at[0]),
        pltpu.make_async_copy(nut, q.at[3, planes, rows, :], load_sem.at[1]),
        pltpu.make_async_copy(bvel, bar.at[0:3], load_sem.at[2]),
        pltpu.make_async_copy(bnut, bar.at[3], load_sem.at[3]),
        pltpu.make_async_copy(mask, mask_v, load_sem.at[4]),
        pltpu.make_async_copy(bins, bin_v, load_sem.at[5]),
        pltpu.make_async_copy(dist, dist_v, load_sem.at[6]),
    ]
    for copy in loads:
        copy.start()

    barrier = pltpu.get_barrier_semaphore()
    for d in range(3):
        for s in range(2):
            @pl.when(has[d][s])
            def _():
                pl.semaphore_signal(barrier, inc=1, device_id=peer[d][s], device_id_type=MESH)

    def remote(src, dst, slot, d, s):
        return pltpu.make_async_remote_copy(
            src_ref=src, dst_ref=dst, send_sem=send_sem.at[slot], recv_sem=recv_sem.at[slot],
            device_id=peer[d][s], device_id_type=MESH,
        )

    first = [[None, None] for _ in range(3)]
    for s in range(2):
        end = (0, cx - 1)[s]
        halo = (cx + 1, 0)[s]
        first[0][s] = [
            remote(vel.at[:, end], q.at[0:3, halo, rows, :], 0 + s, 0, s),
            remote(nut.at[end], q.at[3, halo, rows, :], 2 + s, 0, s),
        ]
        end = (0, cy - 1)[s]
        halo = (PAD + cy, PAD - 1)[s]
        first[1][s] = [
            remote(vel.at[:, :, end, :], q.at[0:3, planes, halo, :], 4 + s, 1, s),
            remote(nut.at[:, end, :], q.at[3, planes, halo, :], 6 + s, 1, s),
        ]
        first[2][s] = [remote(z_send.at[s], z_recv.at[1 - s], 8 + s, 2, s)]
    second = [[None, None] for _ in range(3)]
    for s in range(2):
        end = (1, cx)[s]
        halo = (cx + 1, 0)[s]
        second[0][s] = [remote(nx.at[:, end], nx.at[:, halo], 10 + s, 0, s)]
        end = (PAD, PAD + cy - 1)[s]
        second[1][s] = [remote(ny.at[:, :, end, :], y_halo.at[1 - s], 12 + s, 1, s)]
        second[2][s] = [remote(w_send.at[s], w_recv.at[1 - s], 14 + s, 2, s)]

    def start(copies, d):
        for s in range(2):
            @pl.when(has[d][s])
            def _():
                for copy in copies[d][s]:
                    copy.start()

    def arrive(copies, d):
        for s in range(2):
            @pl.when(has[d][1 - s])
            def _():
                for copy in copies[d][s]:
                    copy.wait_recv()

    def sent(copies, d):
        for s in range(2):
            @pl.when(has[d][s])
            def _():
                for copy in copies[d][s]:
                    copy.wait_send()

    for s in range(2):
        @pl.when(jnp.logical_not(has[0][s]))
        def _():
            halo = (0, cx + 1)[s]
            q[:, halo, rows, :] = jnp.zeros((4, cy, LANES), f32)
            nx[:, halo] = jnp.zeros((4, cy, LANES), f32)

        @pl.when(jnp.logical_not(has[1][s]))
        def _():
            halo = (PAD - 1, PAD + cy)[s]
            for f in range(4):
                q[f, planes, halo, :] = jnp.zeros((cx, LANES), f32)
            y_halo[s] = jnp.zeros((4, cx, LANES), f32)

        @pl.when(jnp.logical_not(has[2][s]))
        def _():
            z_recv[s] = jnp.zeros((4 * groups, LANES), f32)
            w_recv[s] = jnp.zeros((4 * groups, LANES), f32)

    at = lax.broadcasted_iota(jnp.int32, (LANES, LANES), 0)
    to = lax.broadcasted_iota(jnp.int32, (LANES, LANES), 1)
    one = lambda where: jnp.where(where, 1.0, 0.0)
    change = (one(at == to + 1) - one(at == to - 1)).astype(bf16)
    for f in range(4):
        ends = one((at == LANES - 1) & (to == f)) + one((at == 0) & (to == 4 + f))
        for half_of in range(2):
            block = pl.ds(half_of * LANES, LANES)
            pick[f, block, 0:LANES] = change
            pick[f, block, LANES:2 * LANES] = ends.astype(bf16)
    at = lax.broadcasted_iota(jnp.int32, (16, LANES), 0) % 8
    to = lax.broadcasted_iota(jnp.int32, (16, LANES), 1)
    for f in range(4):
        place[:, f * LANES:(f + 1) * LANES] = (
            one((at == 4 + f) & (to == LANES - 1)) - one((at == f) & (to == 0))
        ).astype(bf16)

    def split(value):
        coarse = value.astype(bf16)
        return coarse, (value - coarse.astype(f32)).astype(bf16)

    def set_parts(f, p, value):
        coarse, fine = split(value)
        here = pl.ds(pl.multiple_of(p * cy, cy), cy)
        parts[here, 2 * f * LANES:(2 * f + 1) * LANES] = coarse
        parts[here, (2 * f + 1) * LANES:(2 * f + 2) * LANES] = fine

    def along_z(g, take, dst):
        here = pl.ds(g * LANES, LANES)
        ends = None
        for f in range(4):
            out = jnp.dot(
                parts[here, 2 * f * LANES:(2 * f + 2) * LANES], pick[f],
                preferred_element_type=f32,
            )
            take(f, g, out[:, :LANES].reshape(group, cy, LANES))
            ends = out[:, LANES:] if ends is None else ends + out[:, LANES:]
        turned = ends.T
        dst[1, 4 * g:4 * g + 4, :] = turned[0:4]
        dst[0, 4 * g:4 * g + 4, :] = turned[4:8]

    def add_halo(g, src, take):
        value = jnp.concatenate([src[0, 4 * g:4 * g + 4, :], src[1, 4 * g:4 * g + 4, :]], axis=0)
        coarse = value.astype(bf16).astype(f32)
        both = jnp.concatenate([coarse, value - coarse], axis=0).T.astype(bf16)
        out = jnp.dot(both, place[...], preferred_element_type=f32)
        for f in range(4):
            take(f, g, out[:, f * LANES:(f + 1) * LANES].reshape(group, cy, LANES))

    def set_dz(f, g, value):
        dz[f, g * group:(g + 1) * group] = value

    def add_dz(f, g, value):
        dz[f, g * group:(g + 1) * group] += value

    def add_res(f, g, value):
        if f < 3:
            ovel[f, g * group:(g + 1) * group] += value
        else:
            onut[g * group:(g + 1) * group] += value

    loads[0].wait()
    loads[1].wait()

    def part_plane(p, carry):
        for f in range(4):
            set_parts(f, p, q[f, p + 1, rows, :])
        return carry

    lax.fori_loop(0, cx, part_plane, 0)
    for g in range(groups):
        along_z(g, set_dz, z_send)

    present = sum(h.astype(jnp.int32) for pair in has for h in pair)
    pl.semaphore_wait(barrier, present)
    start(first, 2)
    start(first, 0)
    start(first, 1)

    for copy in loads[2:]:
        copy.wait()
    table = 1.0 / jnp.minimum(dist_v[...], des_length)
    table = table * table * (2.0 * (2.0 * coef_prod / kappa_sq - 2.0 * coef_dest))
    table = jnp.broadcast_to(
        jnp.pad(table, (0, LANES - table.shape[0])).reshape(1, LANES), (8, LANES)
    )

    def look(p, carry):
        for t in range(tiles):
            here = slice(8 * t, 8 * t + 8)
            near[p, here, :] = jnp.take_along_axis(table, bin_v[p, here, :], axis=1)
        return carry

    lax.fori_loop(0, cx, look, 0)

    arrive(first, 2)
    for g in range(groups):
        add_halo(g, z_recv, add_dz)
    arrive(first, 0)
    arrive(first, 1)

    half = 0.5 * step_size

    def plane(p, carry):
        along = [[] for _ in range(4)]
        for t in range(tiles):
            lo = 8 * t
            mid = slice(PAD + lo, PAD + lo + 8)
            up = slice(PAD + lo + 1, PAD + lo + 9)
            down = slice(PAD + lo - 1, PAD + lo + 7)
            here = slice(lo, lo + 8)
            cell = [q[f, p + 1, mid, :] for f in range(4)]
            diff = [
                [
                    q[f, p + 2, mid, :] - q[f, p, mid, :],
                    q[f, p + 1, up, :] - q[f, p + 1, down, :],
                    dz[f, p, here, :],
                ]
                for f in range(4)
            ]
            wet = jnp.where(mask_v[p, here, :] != 0, half, 0.0)
            bars = [bar[i, p, here, :] for i in range(4)]
            scaled = [wet * b for b in bars]
            spin = {
                (0, 1): diff[0][1] - diff[1][0],
                (0, 2): diff[0][2] - diff[2][0],
                (1, 2): diff[1][2] - diff[2][1],
            }
            total = 1.0 + 0.25 * (
                spin[0, 1] * spin[0, 1] + spin[0, 2] * spin[0, 2] + spin[1, 2] * spin[1, 2]
            )
            inverse = lax.rsqrt(total)
            omega = total * inverse
            weight = scaled[3] * cell[3] * inverse * (0.5 * coef_prod)
            flux = [[scaled[i] * cell[j] for j in range(3)] for i in range(4)]
            for (i, j), value in spin.items():
                turn = weight * value
                flux[i][j] = flux[i][j] - turn
                flux[j][i] = flux[j][i] + turn
            for i in range(4):
                nx[i, p + 1, here, :] = flux[i][0]
                ny[i, p, mid, :] = flux[i][1]
                along[i].append(flux[i][2])
            for j in range(3):
                value = bars[j]
                for i in range(4):
                    value = value - scaled[i] * diff[i][j]
                ovel[j, p, here, :] = value
            onut[p, here, :] = bars[3] + scaled[3] * (
                (2.0 * coef_prod) * omega + cell[3] * near[p, here, :]
            )
        for i in range(4):
            set_parts(i, p, jnp.concatenate(along[i], axis=0))
        return carry

    plane(0, 0)
    plane(cx - 1, 0)
    start(second, 0)
    lax.fori_loop(1, cx - 1, plane, 0)
    start(second, 1)
    for g in range(groups):
        along_z(g, add_res, w_send)
    start(second, 2)

    for i in range(4):
        ny[i, :, PAD - 1, :] = jnp.zeros((cx, LANES), f32)
        ny[i, :, PAD + cy, :] = jnp.zeros((cx, LANES), f32)

    def finish(p, carry):
        for t in range(tiles):
            lo = 8 * t
            here = slice(lo, lo + 8)
            up = slice(PAD + lo + 1, PAD + lo + 9)
            down = slice(PAD + lo - 1, PAD + lo + 7)
            for i in range(4):
                value = (nx[i, p + 2, here, :] - nx[i, p, here, :]) + (
                    ny[i, p, up, :] - ny[i, p, down, :]
                )
                if i < 3:
                    ovel[i, p, here, :] += value
                else:
                    onut[p, here, :] += value
        return carry

    lax.fori_loop(1, cx - 1, finish, 0)
    arrive(second, 0)
    finish(0, 0)
    finish(cx - 1, 0)
    arrive(second, 1)
    for i in range(3):
        ovel[i, :, 0, :] -= y_halo[0, i]
        ovel[i, :, cy - 1, :] += y_halo[1, i]
    onut[:, 0, :] -= y_halo[0, 3]
    onut[:, cy - 1, :] += y_halo[1, 3]
    arrive(second, 2)
    for g in range(groups):
        add_halo(g, w_recv, add_res)
    for d in range(3):
        sent(first, d)
        sent(second, d)


def shards(counts, *args):
    velocity, nut_field = args[0], args[1]
    cx, cy, cz = nut_field.shape
    f32 = jnp.float32
    group = LANES // cy
    packed = (2, 4 * (cx // group), LANES)
    hbm = pl.BlockSpec(memory_space=pltpu.HBM)
    vmem = pl.BlockSpec(memory_space=pltpu.VMEM)
    return pl.pallas_call(
        functools.partial(section_kernel, counts),
        out_shape=(
            jax.ShapeDtypeStruct(velocity.shape, f32),
            jax.ShapeDtypeStruct(nut_field.shape, f32),
        ),
        in_specs=[hbm] * 7,
        out_specs=(vmem, vmem),
        scratch_shapes=[
            pltpu.VMEM((4, cx + 2, cy + 2 * PAD, cz), f32),
            pltpu.VMEM((4, cx, cy, cz), f32),
            pltpu.VMEM((cx, cy, cz), jnp.int32),
            pltpu.VMEM((cx, cy, cz), jnp.int32),
            pltpu.VMEM(args[6].shape, f32),
            pltpu.VMEM((cx, cy, cz), f32),
            pltpu.VMEM((4, cx, cy, cz), f32),
            pltpu.VMEM((4, cx + 2, cy, cz), f32),
            pltpu.VMEM((4, cx, cy + 2 * PAD, cz), f32),
            pltpu.VMEM((cx * cy, 8 * LANES), jnp.bfloat16),
            pltpu.VMEM((4, 2 * LANES, 2 * LANES), jnp.bfloat16),
            pltpu.VMEM((16, 4 * LANES), jnp.bfloat16),
            pltpu.VMEM((2, 4, cx, cz), f32),
            pltpu.VMEM(packed, f32),
            pltpu.VMEM(packed, f32),
            pltpu.VMEM(packed, f32),
            pltpu.VMEM(packed, f32),
            pltpu.SemaphoreType.DMA((7,)),
            pltpu.SemaphoreType.DMA((16,)),
            pltpu.SemaphoreType.DMA((16,)),
        ],
        compiler_params=pltpu.CompilerParams(
            collective_id=0, has_side_effects=True, vmem_limit_bytes=32 * 1024 * 1024
        ),
        name="section_adjoint",
    )(*[pltpu.with_memory_space_constraint(x, pltpu.HBM) for x in args])


def solution(mesh):
    counts = tuple(mesh.shape[a] for a in AXES)
    field = P("gx", "gy", "gz")
    tensor = P(None, "gx", "gy", "gz")
    return jax.shard_map(
        functools.partial(shards, counts),
        mesh=mesh,
        in_specs=(tensor, field, tensor, field, field, field, P()),
        out_specs=(tensor, field),
        check_vma=False,
    )
```

time: 39.2 us -> 27.6 us (0.70); the launches traced: 38.6 us -> 27.5 us
  local copies, waits for them, and re-layouts: 8.3 us -> 1.58 us
  Pallas kernels: 29.7 us -> 25.3 us
    unnamed x16 -> x2, local copies, waits for them, and re-layouts: 8.3 us -> 1.58 us
    pallas_call x1, Pallas kernels: 29.7 us -> 25.3 us  [shards(): pl.pallas_call(functools.partial(section_kernel, counts), out_shape=(jax....]
where the time goes in v2:
time: 27.6 us; the launch traced here: 27.5 us
  Pallas kernels  25.3 us (92%)
  local copies, waits for them, and re-layouts  1.58 us (6%)
  between operations  0.64 us (2%)
    pallas_call x1, Pallas kernels, shards(): pl.pallas_call(functools.partial(section_kernel, counts), out_shape=(jax....  25.3 us
    unnamed x2, local copies, waits for them, and re-layouts  1.58 us

profile of v2, /device:TPU:6, one launch (start us, length us, event | category | flops | bytes accessed | tf_op | source)
XLA Modules:
  0.0 27.5 jit_solution(3956899939581029074)
XLA Ops:
  0.6 25.3 %section_adjoint.1 = (f32[3,16,32,128]{3,2,1,0:T(8,128)S(1)}, f32[16,32,128]{2,1,0:T(8,128)S(1)}) custom-call(f32[3,16,32,128]{3,2,1,0:T(8,128)} %vel.1, f32[16,32,128]{2,1,0:T(8,128)} %nut.1, f32[3,16,32,128]{3,2,1,0:T(8,128)} %bvel.1, f32[16,32,128]{2,1,0:T(8,128)} %bnut.1, s32[16,32,128]{2,1,0:T(8,128)} %bins.1, s32[16,32,128]{2,1,0:T(8,128)} %mask.1, f32[32]{0:T(128)} %dist.1), custom_call_target="tpu_custom_call" | custom-call | tf_op jit(solution)/shard_map/section_adjoint/pallas_call | solution.py:338
  25.9 0.9 %copy.11 = f32[3,16,32,128]{3,2,1,0:T(8,128)} copy(f32[3,16,32,128]{3,2,1,0:T(8,128)S(1)} %get-tuple-element.4) | data formatting | bytes 1572864
  26.8 0.7 %copy.12 = f32[16,32,128]{2,1,0:T(8,128)} copy(f32[16,32,128]{2,1,0:T(8,128)S(1)} %get-tuple-element.5) | data formatting | bytes 524288

commit v3 on v2

--- a/solution.py
+++ b/solution.py
@@ -15,6 +15,7 @@
 
 MESH = pl.DeviceIdType.MESH
 AXES = ("gx", "gy", "gz")
+GREET = (1, 0, 0)
 PAD = 8
 LANES = 128
 
@@ -22,7 +23,7 @@
 def section_kernel(
     counts, vel, nut, bvel, bnut, bins, mask, dist, ovel, onut,
     q, bar, bin_v, mask_v, dist_v, near, dz, nx, ny, parts, pick, place, y_halo,
-    z_send, z_recv, w_send, w_recv, load_sem, send_sem, recv_sem,
+    x_halo, z_send, z_recv, w_send, w_recv, load_sem, send_sem, recv_sem, ready,
 ):
     cx, cy = nut.shape[0], nut.shape[1]
     tiles = cy // 8
@@ -35,6 +36,14 @@
     pos = [lax.axis_index(a) for a in AXES]
     has = [(pos[d] > 0, pos[d] < counts[d] - 1) for d in range(3)]
     peer = [({AXES[d]: pos[d] - 1}, {AXES[d]: pos[d] + 1}) for d in range(3)]
+
+    barrier = pltpu.get_barrier_semaphore()
+    for d in range(3):
+        @pl.when(has[d][1 - GREET[d]])
+        def _():
+            pl.semaphore_signal(
+                barrier, inc=1, device_id=peer[d][1 - GREET[d]], device_id_type=MESH
+            )
 
     loads = [
         pltpu.make_async_copy(vel, q.at[0:3, planes, rows, :], load_sem.at[0]),
@@ -48,13 +57,6 @@
     for copy in loads:
         copy.start()
 
-    barrier = pltpu.get_barrier_semaphore()
-    for d in range(3):
-        for s in range(2):
-            @pl.when(has[d][s])
-            def _():
-                pl.semaphore_signal(barrier, inc=1, device_id=peer[d][s], device_id_type=MESH)
-
     def remote(src, dst, slot, d, s):
         return pltpu.make_async_remote_copy(
             src_ref=src, dst_ref=dst, send_sem=send_sem.at[slot], recv_sem=recv_sem.at[slot],
@@ -62,12 +64,15 @@
         )
 
     first = [[None, None] for _ in range(3)]
+    late = [[None, None]]
+    plain = [[None, None]]
     for s in range(2):
         end = (0, cx - 1)[s]
         halo = (cx + 1, 0)[s]
-        first[0][s] = [
-            remote(vel.at[:, end], q.at[0:3, halo, rows, :], 0 + s, 0, s),
-            remote(nut.at[end], q.at[3, halo, rows, :], 2 + s, 0, s),
+        first[0][s] = [remote(vel.at[1:3, end], q.at[1:3, halo, rows, :], 0 + s, 0, s)]
+        late[0][s] = [
+            remote(vel.at[0, end], x_halo.at[1 - s, 0], 2 + s, 0, s),
+            remote(nut.at[end], x_halo.at[1 - s, 1], 16 + s, 0, s),
         ]
         end = (0, cy - 1)[s]
         halo = (PAD + cy, PAD - 1)[s]
@@ -80,24 +85,26 @@
     for s in range(2):
         end = (1, cx)[s]
         halo = (cx + 1, 0)[s]
-        second[0][s] = [remote(nx.at[:, end], nx.at[:, halo], 10 + s, 0, s)]
+        plain[0][s] = [
+            remote(nx.at[0, end], nx.at[0, halo], 18 + s, 0, s),
+            remote(nx.at[3, end], nx.at[3, halo], 20 + s, 0, s),
+        ]
+        second[0][s] = [remote(nx.at[1:3, end], nx.at[1:3, halo], 10 + s, 0, s)]
         end = (PAD, PAD + cy - 1)[s]
         second[1][s] = [remote(ny.at[:, :, end, :], y_halo.at[1 - s], 12 + s, 1, s)]
         second[2][s] = [remote(w_send.at[s], w_recv.at[1 - s], 14 + s, 2, s)]
 
-    def start(copies, d):
-        for s in range(2):
-            @pl.when(has[d][s])
-            def _():
-                for copy in copies[d][s]:
-                    copy.start()
-
-    def arrive(copies, d):
-        for s in range(2):
-            @pl.when(has[d][1 - s])
-            def _():
-                for copy in copies[d][s]:
-                    copy.wait_recv()
+    def start(copies, d, s):
+        @pl.when(has[d][s])
+        def _():
+            for copy in copies[d][s]:
+                copy.start()
+
+    def arrive(copies, d, side):
+        @pl.when(has[d][side])
+        def _():
+            for copy in copies[d][1 - side]:
+                copy.wait_recv()
 
     def sent(copies, d):
         for s in range(2):
@@ -106,11 +113,15 @@
                 for copy in copies[d][s]:
                     copy.wait_send()
 
+    for f in (0, 3):
+        for halo in (0, cx + 1):
+            q[f, halo, rows, :] = jnp.zeros((cy, LANES), f32)
     for s in range(2):
         @pl.when(jnp.logical_not(has[0][s]))
         def _():
             halo = (0, cx + 1)[s]
-            q[:, halo, rows, :] = jnp.zeros((4, cy, LANES), f32)
+            q[1:3, halo, rows, :] = jnp.zeros((2, cy, LANES), f32)
+            x_halo[s] = jnp.zeros((2, cy, LANES), f32)
             nx[:, halo] = jnp.zeros((4, cy, LANES), f32)
 
         @pl.when(jnp.logical_not(has[1][s]))
@@ -122,7 +133,6 @@
 
         @pl.when(jnp.logical_not(has[2][s]))
         def _():
-            z_recv[s] = jnp.zeros((4 * groups, LANES), f32)
             w_recv[s] = jnp.zeros((4 * groups, LANES), f32)
 
     at = lax.broadcasted_iota(jnp.int32, (LANES, LANES), 0)
@@ -152,22 +162,32 @@
         parts[here, 2 * f * LANES:(2 * f + 1) * LANES] = coarse
         parts[here, (2 * f + 1) * LANES:(2 * f + 2) * LANES] = fine
 
-    def along_z(g, take, dst):
+    def along_z(g, take, dst, sides):
         here = pl.ds(g * LANES, LANES)
         ends = None
         for f in range(4):
-            out = jnp.dot(
-                parts[here, 2 * f * LANES:(2 * f + 2) * LANES], pick[f],
-                preferred_element_type=f32,
-            )
-            take(f, g, out[:, :LANES].reshape(group, cy, LANES))
-            ends = out[:, LANES:] if ends is None else ends + out[:, LANES:]
+            part = parts[here, 2 * f * LANES:(2 * f + 2) * LANES]
+            if take is None:
+                out = jnp.dot(part, pick[f, :, LANES:], preferred_element_type=f32)
+            else:
+                out = jnp.dot(part, pick[f], preferred_element_type=f32)
+                take(f, g, out[:, :LANES].reshape(group, cy, LANES))
+                out = out[:, LANES:]
+            ends = out if ends is None else ends + out
         turned = ends.T
-        dst[1, 4 * g:4 * g + 4, :] = turned[0:4]
-        dst[0, 4 * g:4 * g + 4, :] = turned[4:8]
-
-    def add_halo(g, src, take):
-        value = jnp.concatenate([src[0, 4 * g:4 * g + 4, :], src[1, 4 * g:4 * g + 4, :]], axis=0)
+        if 1 in sides:
+            dst[1, 4 * g:4 * g + 4, :] = turned[0:4]
+        if 0 in sides:
+            dst[0, 4 * g:4 * g + 4, :] = turned[4:8]
+
+    def add_halo(g, src, take, sides):
+        value = jnp.concatenate(
+            [
+                src[s, 4 * g:4 * g + 4, :] if s in sides else jnp.zeros((4, LANES), f32)
+                for s in range(2)
+            ],
+            axis=0,
+        )
         coarse = value.astype(bf16).astype(f32)
         both = jnp.concatenate([coarse, value - coarse], axis=0).T.astype(bf16)
         out = jnp.dot(both, place[...], preferred_element_type=f32)
@@ -196,15 +216,32 @@
 
     lax.fori_loop(0, cx, part_plane, 0)
     for g in range(groups):
-        along_z(g, set_dz, z_send)
-
-    present = sum(h.astype(jnp.int32) for pair in has for h in pair)
-    pl.semaphore_wait(barrier, present)
-    start(first, 2)
-    start(first, 0)
-    start(first, 1)
-
-    for copy in loads[2:]:
+        along_z(g, set_dz, z_send, (0, 1))
+
+    present = sum(has[d][GREET[d]].astype(jnp.int32) for d in range(3))
+    @pl.when(present > 0)
+    def _():
+        pl.semaphore_wait(barrier, present)
+
+    for d in (2, 0, 1):
+        @pl.when(has[d][GREET[d]])
+        def _():
+            pl.semaphore_signal(
+                ready.at[d], inc=1, device_id=peer[d][GREET[d]], device_id_type=MESH
+            )
+    for d in (2, 0, 1):
+        start(first, d, GREET[d])
+
+    for copy in loads[2:5]:
+        copy.wait()
+    half = 0.5 * step_size
+    for p in (0, cx - 1):
+        wet = jnp.where(mask_v[p] != 0, half, 0.0)
+        for i in (0, 3):
+            nx[i, p + 1] = wet * bar[i, p] * q[0, p + 1, rows, :]
+    start(plain, 0, GREET[0])
+    start(late, 0, GREET[0])
+    for copy in loads[5:]:
         copy.wait()
     table = 1.0 / jnp.minimum(dist_v[...], des_length)
     table = table * table * (2.0 * (2.0 * coef_prod / kappa_sq - 2.0 * coef_dest))
@@ -220,15 +257,20 @@
 
     lax.fori_loop(0, cx, look, 0)
 
-    arrive(first, 2)
-    for g in range(groups):
-        add_halo(g, z_recv, add_dz)
-    arrive(first, 0)
-    arrive(first, 1)
-
-    half = 0.5 * step_size
-
-    def plane(p, carry):
+    for d in (1, 0, 2):
+        @pl.when(has[d][1 - GREET[d]])
+        def _():
+            pl.semaphore_wait(ready.at[d], 1)
+        start(first, d, 1 - GREET[d])
+        if d == 0:
+            start(plain, 0, 1 - GREET[0])
+            start(late, 0, 1 - GREET[0])
+
+    for d in (1, 0):
+        for side in range(2):
+            arrive(first, d, side)
+
+    def plane(p, carry, inner=True, brief=False):
         along = [[] for _ in range(4)]
         for t in range(tiles):
             lo = 8 * t
@@ -264,8 +306,13 @@
                 turn = weight * value
                 flux[i][j] = flux[i][j] - turn
                 flux[j][i] = flux[j][i] + turn
+            if brief:
+                for i in range(4):
+                    along[i].append(flux[i][2])
+                continue
             for i in range(4):
-                nx[i, p + 1, here, :] = flux[i][0]
+                if i in (1, 2) or inner:
+                    nx[i, p + 1, here, :] = flux[i][0]
                 ny[i, p, mid, :] = flux[i][1]
                 along[i].append(flux[i][2])
             for j in range(3):
@@ -280,14 +327,32 @@
             set_parts(i, p, jnp.concatenate(along[i], axis=0))
         return carry
 
-    plane(0, 0)
-    plane(cx - 1, 0)
-    start(second, 0)
+    @pl.when(has[2][0])
+    def _():
+        arrive(first, 2, 0)
+        for g in range(groups):
+            add_halo(g, z_recv, add_dz, (0,))
+        lax.fori_loop(0, cx, functools.partial(plane, brief=True), 0)
+        for g in range(groups):
+            along_z(g, None, w_send, (0,))
+        start(second, 2, 0)
+
+    @pl.when(has[2][1])
+    def _():
+        arrive(first, 2, 1)
+        for g in range(groups):
+            add_halo(g, z_recv, add_dz, (1,))
+
+    plane(0, 0, False)
+    plane(cx - 1, 0, False)
+    for s in range(2):
+        start(second, 0, s)
     lax.fori_loop(1, cx - 1, plane, 0)
-    start(second, 1)
+    for s in range(2):
+        start(second, 1, s)
     for g in range(groups):
-        along_z(g, add_res, w_send)
-    start(second, 2)
+        along_z(g, add_res, w_send, (1,))
+    start(second, 2, 1)
 
     for i in range(4):
         ny[i, :, PAD - 1, :] = jnp.zeros((cx, LANES), f32)
@@ -310,21 +375,44 @@
         return carry
 
     lax.fori_loop(1, cx - 1, finish, 0)
-    arrive(second, 0)
-    finish(0, 0)
-    finish(cx - 1, 0)
-    arrive(second, 1)
+    for side in range(2):
+        arrive(late, 0, side)
+        arrive(plain, 0, side)
+        arrive(second, 1, side)
+    for s in range(2):
+        p = (0, cx - 1)[s]
+        wet = jnp.where(mask_v[p] != 0, (half, -half)[s], 0.0)
+        ovel[0, p] += wet * (bar[0, p] * x_halo[s, 0] + bar[3, p] * x_halo[s, 1])
     for i in range(3):
         ovel[i, :, 0, :] -= y_halo[0, i]
         ovel[i, :, cy - 1, :] += y_halo[1, i]
     onut[:, 0, :] -= y_halo[0, 3]
     onut[:, cy - 1, :] += y_halo[1, 3]
-    arrive(second, 2)
-    for g in range(groups):
-        add_halo(g, w_recv, add_res)
     for d in range(3):
         sent(first, d)
+    sent(late, 0)
+    sent(plain, 0)
+    for side in range(2):
+        arrive(second, 0, side)
+    finish(0, 0)
+    finish(cx - 1, 0)
+    for side in range(2):
+        arrive(second, 2, side)
+    for g in range(groups):
+        add_halo(g, w_recv, add_res, (0, 1))
+    for d in range(3):
         sent(second, d)
+
+
+def out_kernel(vel_in, nut_in, vel_out, nut_out, sem):
+    copies = [
+        pltpu.make_async_copy(vel_in, vel_out, sem.at[0]),
+        pltpu.make_async_copy(nut_in, nut_out, sem.at[1]),
+    ]
+    for copy in copies:
+        copy.start()
+    for copy in copies:
+        copy.wait()
 
 
 def shards(counts, *args):
@@ -335,7 +423,7 @@
     packed = (2, 4 * (cx // group), LANES)
     hbm = pl.BlockSpec(memory_space=pltpu.HBM)
     vmem = pl.BlockSpec(memory_space=pltpu.VMEM)
-    return pl.pallas_call(
+    result = pl.pallas_call(
         functools.partial(section_kernel, counts),
         out_shape=(
             jax.ShapeDtypeStruct(velocity.shape, f32),
@@ -357,19 +445,32 @@
             pltpu.VMEM((4, 2 * LANES, 2 * LANES), jnp.bfloat16),
             pltpu.VMEM((16, 4 * LANES), jnp.bfloat16),
             pltpu.VMEM((2, 4, cx, cz), f32),
+            pltpu.VMEM((2, 2, cy, cz), f32),
             pltpu.VMEM(packed, f32),
             pltpu.VMEM(packed, f32),
             pltpu.VMEM(packed, f32),
             pltpu.VMEM(packed, f32),
             pltpu.SemaphoreType.DMA((7,)),
-            pltpu.SemaphoreType.DMA((16,)),
-            pltpu.SemaphoreType.DMA((16,)),
+            pltpu.SemaphoreType.DMA((22,)),
+            pltpu.SemaphoreType.DMA((22,)),
+            pltpu.SemaphoreType.REGULAR((3,)),
         ],
         compiler_params=pltpu.CompilerParams(
             collective_id=0, has_side_effects=True, vmem_limit_bytes=32 * 1024 * 1024
         ),
         name="section_adjoint",
     )(*[pltpu.with_memory_space_constraint(x, pltpu.HBM) for x in args])
+    return pl.pallas_call(
+        out_kernel,
+        out_shape=(
+            jax.ShapeDtypeStruct(velocity.shape, f32),
+            jax.ShapeDtypeStruct(nut_field.shape, f32),
+        ),
+        in_specs=[vmem] * 2,
+        out_specs=(hbm, hbm),
+        scratch_shapes=[pltpu.SemaphoreType.DMA((2,))],
+        name="section_result",
+    )(*[pltpu.with_memory_space_constraint(x, pltpu.VMEM) for x in result])
 
 
 def solution(mesh):

time: 27.6 us -> 23.4 us (0.85)
  the two profiles are of different devices: /device:TPU:6 before, /device:TPU:62 now
where the time goes in v3:
time: 23.4 us; the launch traced here: 23.3 us
  Pallas kernels  22.6 us (97%)
  between operations  0.64 us (3%)
    pallas_call x1, Pallas kernels, shards(): pl.pallas_call(functools.partial(section_kernel, counts), out_shape=(jax....  21.7 us
    pallas_call x1, Pallas kernels, shards(): pl.pallas_call(out_kernel, out_shape=(jax.ShapeDtypeStruct(velocity.shape...  0.98 us

profile of v3, /device:TPU:62, one launch (start us, length us, event | category | flops | bytes accessed | tf_op | source)
XLA Modules:
  0.0 23.3 jit_solution(14432349421937761156)
XLA Ops:
  0.6 21.7 %section_adjoint.1 = (f32[3,16,32,128]{3,2,1,0:T(8,128)S(1)}, f32[16,32,128]{2,1,0:T(8,128)S(1)}) custom-call(f32[3,16,32,128]{3,2,1,0:T(8,128)} %vel.1, f32[16,32,128]{2,1,0:T(8,128)} %nut.1, f32[3,16,32,128]{3,2,1,0:T(8,128)} %bvel.1, f32[16,32,128]{2,1,0:T(8,128)} %bnut.1, s32[16,32,128]{2,1,0:T(8,128)} %bins.1, s32[16,32,128]{2,1,0:T(8,128)} %mask.1, f32[32]{0:T(128)} %dist.1), custom_call_target="tpu_custom_call" | custom-call | tf_op jit(solution)/shard_map/section_adjoint/pallas_call | solution.py:426
  22.3 1.0 %section_result.1 = (f32[3,16,32,128]{3,2,1,0:T(8,128)}, f32[16,32,128]{2,1,0:T(8,128)}) custom-call(f32[3,16,32,128]{3,2,1,0:T(8,128)S(1)} %get-tuple-element.4.vel_in, f32[16,32,128]{2,1,0:T(8,128)S(1)} %get-tuple-element.5.nut_in), custom_call_target="tpu_custom_call" | custom-call | tf_op jit(solution)/shard_map/section_result/pallas_call | solution.py:463

commit v4 on v3

--- a/solution.py
+++ b/solution.py
@@ -15,7 +15,7 @@
 
 MESH = pl.DeviceIdType.MESH
 AXES = ("gx", "gy", "gz")
-GREET = (1, 0, 0)
+RUN = 4
 PAD = 8
 LANES = 128
 
@@ -23,7 +23,8 @@
 def section_kernel(
     counts, vel, nut, bvel, bnut, bins, mask, dist, ovel, onut,
     q, bar, bin_v, mask_v, dist_v, near, dz, nx, ny, parts, pick, place, y_halo,
-    x_halo, z_send, z_recv, w_send, w_recv, load_sem, send_sem, recv_sem, ready,
+    x_halo, z_send, z_recv, w_recv, own, own_recv, cross, cross_recv,
+    load_sem, send_sem, recv_sem, ready,
 ):
     cx, cy = nut.shape[0], nut.shape[1]
     tiles = cy // 8
@@ -38,12 +39,26 @@
     peer = [({AXES[d]: pos[d] - 1}, {AXES[d]: pos[d] + 1}) for d in range(3)]
 
     barrier = pltpu.get_barrier_semaphore()
+    first_of_run = lax.rem(pos[0], RUN) == 0
+    last_of_run = lax.rem(pos[0], RUN) == RUN - 1
+    upper = 2 * pos[2] >= counts[2]
+    upper_low = 2 * (pos[2] - 1) >= counts[2]
+    not_ = jnp.logical_not
+    greeted = [
+        (has[0][0] & (not_(first_of_run) | upper), has[0][1] & (last_of_run | upper)),
+        (has[1][0], has[1][1] & upper),
+        (has[2][0], has[2][1] & upper),
+    ]
+    greets = [
+        (has[0][0] & (first_of_run | upper), has[0][1] & (not_(last_of_run) | upper)),
+        (has[1][0] & upper, has[1][1]),
+        (has[2][0] & upper_low, has[2][1]),
+    ]
     for d in range(3):
-        @pl.when(has[d][1 - GREET[d]])
-        def _():
-            pl.semaphore_signal(
-                barrier, inc=1, device_id=peer[d][1 - GREET[d]], device_id_type=MESH
-            )
+        for s in range(2):
+            @pl.when(greets[d][s])
+            def _():
+                pl.semaphore_signal(barrier, inc=1, device_id=peer[d][s], device_id_type=MESH)
 
     loads = [
         pltpu.make_async_copy(vel, q.at[0:3, planes, rows, :], load_sem.at[0]),
@@ -81,6 +96,7 @@
             remote(nut.at[:, end, :], q.at[3, planes, halo, :], 6 + s, 1, s),
         ]
         first[2][s] = [remote(z_send.at[s], z_recv.at[1 - s], 8 + s, 2, s)]
+    middle = [None, None, [None, None]]
     second = [[None, None] for _ in range(3)]
     for s in range(2):
         end = (1, cx)[s]
@@ -92,10 +108,11 @@
         second[0][s] = [remote(nx.at[1:3, end], nx.at[1:3, halo], 10 + s, 0, s)]
         end = (PAD, PAD + cy - 1)[s]
         second[1][s] = [remote(ny.at[:, :, end, :], y_halo.at[1 - s], 12 + s, 1, s)]
-        second[2][s] = [remote(w_send.at[s], w_recv.at[1 - s], 14 + s, 2, s)]
-
-    def start(copies, d, s):
-        @pl.when(has[d][s])
+        middle[2][s] = [remote(own.at[s], own_recv.at[1 - s], 22 + s, 2, s)]
+        second[2][s] = [remote(cross.at[s], cross_recv.at[1 - s], 14 + s, 2, s)]
+
+    def start(copies, d, s, where):
+        @pl.when(where[d][s])
         def _():
             for copy in copies[d][s]:
                 copy.start()
@@ -162,23 +179,28 @@
         parts[here, 2 * f * LANES:(2 * f + 1) * LANES] = coarse
         parts[here, (2 * f + 1) * LANES:(2 * f + 2) * LANES] = fine
 
-    def along_z(g, take, dst, sides):
+    def along_z(g, take, dst, sides, count=4, base=0):
         here = pl.ds(g * LANES, LANES)
         ends = None
-        for f in range(4):
+        for f in range(count):
             part = parts[here, 2 * f * LANES:(2 * f + 2) * LANES]
             if take is None:
                 out = jnp.dot(part, pick[f, :, LANES:], preferred_element_type=f32)
+            elif not sides:
+                out = jnp.dot(part, pick[f, :, :LANES], preferred_element_type=f32)
+                take(f, g, out.reshape(group, cy, LANES))
+                continue
             else:
                 out = jnp.dot(part, pick[f], preferred_element_type=f32)
                 take(f, g, out[:, :LANES].reshape(group, cy, LANES))
                 out = out[:, LANES:]
             ends = out if ends is None else ends + out
+        if not sides:
+            return
         turned = ends.T
-        if 1 in sides:
-            dst[1, 4 * g:4 * g + 4, :] = turned[0:4]
-        if 0 in sides:
-            dst[0, 4 * g:4 * g + 4, :] = turned[4:8]
+        at_row = base + 4 * g
+        for s in sides:
+            dst[s, at_row:at_row + 4, :] = (turned[4:8], turned[0:4])[s]
 
     def add_halo(g, src, take, sides):
         value = jnp.concatenate(
@@ -206,6 +228,24 @@
         else:
             onut[g * group:(g + 1) * group] += value
 
+    present = sum(g.astype(jnp.int32) for pair in greeted for g in pair)
+
+    @pl.when(present > 0)
+    def _():
+        pl.semaphore_wait(barrier, present)
+
+    for d in (2, 0, 1):
+        for s in range(2):
+            @pl.when(greeted[d][s] & not_(greets[d][s]))
+            def _():
+                pl.semaphore_signal(
+                    ready.at[d, 1 - s], inc=1, device_id=peer[d][s], device_id_type=MESH
+                )
+    for s in range(2):
+        start(first, 0, s, greeted)
+    for s in range(2):
+        start(first, 1, s, greeted)
+
     loads[0].wait()
     loads[1].wait()
 
@@ -218,19 +258,19 @@
     for g in range(groups):
         along_z(g, set_dz, z_send, (0, 1))
 
-    present = sum(has[d][GREET[d]].astype(jnp.int32) for d in range(3))
-    @pl.when(present > 0)
-    def _():
-        pl.semaphore_wait(barrier, present)
-
-    for d in (2, 0, 1):
-        @pl.when(has[d][GREET[d]])
-        def _():
-            pl.semaphore_signal(
-                ready.at[d], inc=1, device_id=peer[d][GREET[d]], device_id_type=MESH
-            )
-    for d in (2, 0, 1):
-        start(first, d, GREET[d])
+    for s in range(2):
+        start(first, 2, s, greeted)
+
+    def told(d, s, copies):
+        @pl.when(has[d][s] & not_(greeted[d][s]))
+        def _():
+            pl.semaphore_wait(ready.at[d, s], 1)
+            for copy in copies:
+                copy.start()
+
+    told(1, 1, first[1][1])
+    for s in (1, 0):
+        told(0, s, first[0][s])
 
     for copy in loads[2:5]:
         copy.wait()
@@ -239,8 +279,9 @@
         wet = jnp.where(mask_v[p] != 0, half, 0.0)
         for i in (0, 3):
             nx[i, p + 1] = wet * bar[i, p] * q[0, p + 1, rows, :]
-    start(plain, 0, GREET[0])
-    start(late, 0, GREET[0])
+    for s in range(2):
+        start(plain, 0, s, has)
+        start(late, 0, s, has)
     for copy in loads[5:]:
         copy.wait()
     table = 1.0 / jnp.minimum(dist_v[...], des_length)
@@ -257,20 +298,71 @@
 
     lax.fori_loop(0, cx, look, 0)
 
-    for d in (1, 0, 2):
-        @pl.when(has[d][1 - GREET[d]])
-        def _():
-            pl.semaphore_wait(ready.at[d], 1)
-        start(first, d, 1 - GREET[d])
-        if d == 0:
-            start(plain, 0, 1 - GREET[0])
-            start(late, 0, 1 - GREET[0])
+    def extract(value, count, dst, base=0):
+        def body(p, carry):
+            for f in range(count):
+                set_parts(f, p, value(f, p))
+            return carry
+
+        lax.fori_loop(0, cx, body, 0)
+        for g in range(groups):
+            along_z(g, None, dst, (0, 1), count, base)
+
+    def wet_bar(f, p):
+        return jnp.where(mask_v[p] != 0, half, 0.0) * bar[f, p]
+
+    def own_value(f, p):
+        if f == 0:
+            return wet_bar(3, p) * q[3, p + 1, rows, :] * (0.5 * coef_prod)
+        return dz[f - 1, p]
+
+    above, below = pl.ds(PAD + 1, cy), pl.ds(PAD - 1, cy)
+
+    def cross_value(f, p):
+        if f == 0:
+            return q[2, p + 2, rows, :] - q[2, p, rows, :]
+        if f == 1:
+            return q[2, p + 1, above, :] - q[2, p + 1, below, :]
+        return (q[0, p + 1, above, :] - q[0, p + 1, below, :]) - (
+            q[1, p + 2, rows, :] - q[1, p, rows, :]
+        )
+
+    extract(lambda f, p: wet_bar(f, p) * q[2, p + 1, rows, :], 4, own)
+    extract(own_value, 3, own, 4 * groups)
+    for s in range(2):
+        start(middle, 2, s, greeted)
 
     for d in (1, 0):
         for side in range(2):
             arrive(first, d, side)
-
-    def plane(p, carry, inner=True, brief=False):
+    extract(cross_value, 3, cross)
+    for s in range(2):
+        start(second, 2, s, greeted)
+    told(2, 1, first[2][1] + middle[2][1] + second[2][1])
+
+    def z_flux(side):
+        take = lambda ref, f, base=0: ref[side, pl.ds(base + f, groups, stride=4), :]
+        sign = (1.0, -1.0)[side]
+        more = 4 * groups
+        spin_02, spin_12 = [
+            take(own_recv, 1 + f, more) + sign * take(z_send, f) - take(cross_recv, f)
+            for f in range(2)
+        ]
+        spin_01 = take(cross_recv, 2)
+        total = 1.0 + 0.25 * (spin_01 * spin_01 + spin_02 * spin_02 + spin_12 * spin_12)
+        weight = take(own_recv, 0, more) * lax.rsqrt(total)
+        turns = (weight * spin_02, weight * spin_12, 0.0, 0.0)
+        for f in range(4):
+            w_recv[side, pl.ds(f, groups, stride=4), :] = take(own_recv, f) - turns[f]
+
+    for side in range(2):
+        @pl.when(has[2][side])
+        def _():
+            arrive(first, 2, side)
+            for g in range(groups):
+                add_halo(g, z_recv, add_dz, (side,))
+
+    def plane(p, carry, inner=True):
         along = [[] for _ in range(4)]
         for t in range(tiles):
             lo = 8 * t
@@ -306,10 +398,6 @@
                 turn = weight * value
                 flux[i][j] = flux[i][j] - turn
                 flux[j][i] = flux[j][i] + turn
-            if brief:
-                for i in range(4):
-                    along[i].append(flux[i][2])
-                continue
             for i in range(4):
                 if i in (1, 2) or inner:
                     nx[i, p + 1, here, :] = flux[i][0]
@@ -327,32 +415,15 @@
             set_parts(i, p, jnp.concatenate(along[i], axis=0))
         return carry
 
-    @pl.when(has[2][0])
-    def _():
-        arrive(first, 2, 0)
-        for g in range(groups):
-            add_halo(g, z_recv, add_dz, (0,))
-        lax.fori_loop(0, cx, functools.partial(plane, brief=True), 0)
-        for g in range(groups):
-            along_z(g, None, w_send, (0,))
-        start(second, 2, 0)
-
-    @pl.when(has[2][1])
-    def _():
-        arrive(first, 2, 1)
-        for g in range(groups):
-            add_halo(g, z_recv, add_dz, (1,))
-
     plane(0, 0, False)
     plane(cx - 1, 0, False)
     for s in range(2):
-        start(second, 0, s)
+        start(second, 0, s, has)
     lax.fori_loop(1, cx - 1, plane, 0)
     for s in range(2):
-        start(second, 1, s)
+        start(second, 1, s, has)
     for g in range(groups):
-        along_z(g, add_res, w_send, (1,))
-    start(second, 2, 1)
+        along_z(g, add_res, None, ())
 
     for i in range(4):
         ny[i, :, PAD - 1, :] = jnp.zeros((cx, LANES), f32)
@@ -397,9 +468,15 @@
     finish(0, 0)
     finish(cx - 1, 0)
     for side in range(2):
-        arrive(second, 2, side)
+        @pl.when(has[2][side])
+        def _():
+            arrive(middle, 2, side)
+            arrive(second, 2, side)
+            z_flux(side)
+
     for g in range(groups):
         add_halo(g, w_recv, add_res, (0, 1))
+    sent(middle, 2)
     for d in range(3):
         sent(second, d)
 
@@ -449,11 +526,14 @@
             pltpu.VMEM(packed, f32),
             pltpu.VMEM(packed, f32),
             pltpu.VMEM(packed, f32),
+            pltpu.VMEM((2, 2 * packed[1], LANES), f32),
+            pltpu.VMEM((2, 2 * packed[1], LANES), f32),
+            pltpu.VMEM(packed, f32),
             pltpu.VMEM(packed, f32),
             pltpu.SemaphoreType.DMA((7,)),
-            pltpu.SemaphoreType.DMA((22,)),
-            pltpu.SemaphoreType.DMA((22,)),
-            pltpu.SemaphoreType.REGULAR((3,)),
+            pltpu.SemaphoreType.DMA((24,)),
+            pltpu.SemaphoreType.DMA((24,)),
+            pltpu.SemaphoreType.REGULAR((3, 2)),
         ],
         compiler_params=pltpu.CompilerParams(
             collective_id=0, has_side_effects=True, vmem_limit_bytes=32 * 1024 * 1024

time: 23.4 us -> 22.2 us (0.949)
  the two profiles are of different devices: /device:TPU:62 before, /device:TPU:6 now
where the time goes in v4:
time: 22.2 us; the launch traced here: 22.1 us
  Pallas kernels  21.4 us (96%)
  between operations  0.64 us (3%)
    pallas_call x1, Pallas kernels, shards(): pl.pallas_call(functools.partial(section_kernel, counts), out_shape=(jax....  20.5 us
    pallas_call x1, Pallas kernels, shards(): pl.pallas_call(out_kernel, out_shape=(jax.ShapeDtypeStruct(velocity.shape...  0.98 us

profile of v4, /device:TPU:6, one launch (start us, length us, event | category | flops | bytes accessed | tf_op | source)
XLA Modules:
  0.0 22.1 jit_solution(10651012555283356492)
XLA Ops:
  0.6 20.5 %section_adjoint.1 = (f32[3,16,32,128]{3,2,1,0:T(8,128)S(1)}, f32[16,32,128]{2,1,0:T(8,128)S(1)}) custom-call(f32[3,16,32,128]{3,2,1,0:T(8,128)} %vel.1, f32[16,32,128]{2,1,0:T(8,128)} %nut.1, f32[3,16,32,128]{3,2,1,0:T(8,128)} %bvel.1, f32[16,32,128]{2,1,0:T(8,128)} %bnut.1, s32[16,32,128]{2,1,0:T(8,128)} %bins.1, s32[16,32,128]{2,1,0:T(8,128)} %mask.1, f32[32]{0:T(128)} %dist.1), custom_call_target="tpu_custom_call" | custom-call | tf_op jit(solution)/shard_map/section_adjoint/pallas_call | solution.py:503
  21.1 1.0 %section_result.1 = (f32[3,16,32,128]{3,2,1,0:T(8,128)}, f32[16,32,128]{2,1,0:T(8,128)}) custom-call(f32[3,16,32,128]{3,2,1,0:T(8,128)S(1)} %get-tuple-element.4.vel_in, f32[16,32,128]{2,1,0:T(8,128)S(1)} %get-tuple-element.5.nut_in), custom_call_target="tpu_custom_call" | custom-call | tf_op jit(solution)/shard_map/section_result/pallas_call | solution.py:543

commit v5 on v4

--- a/solution.py
+++ b/solution.py
@@ -69,7 +69,7 @@
         pltpu.make_async_copy(bins, bin_v, load_sem.at[5]),
         pltpu.make_async_copy(dist, dist_v, load_sem.at[6]),
     ]
-    for copy in loads:
+    for copy in loads[:2]:
         copy.start()
 
     def remote(src, dst, slot, d, s):
@@ -248,6 +248,8 @@
 
     loads[0].wait()
     loads[1].wait()
+    for copy in loads[2:]:
+        copy.start()
 
     def part_plane(p, carry):
         for f in range(4):
@@ -256,7 +258,7 @@
 
     lax.fori_loop(0, cx, part_plane, 0)
     for g in range(groups):
-        along_z(g, set_dz, z_send, (0, 1))
+        along_z(g, None, z_send, (0, 1))
 
     for s in range(2):
         start(first, 2, s, greeted)
@@ -271,6 +273,9 @@
     told(1, 1, first[1][1])
     for s in (1, 0):
         told(0, s, first[0][s])
+
+    for g in range(groups):
+        along_z(g, set_dz, None, ())
 
     for copy in loads[2:5]:
         copy.wait()
@@ -359,7 +364,7 @@
         @pl.when(has[2][side])
         def _():
             arrive(first, 2, side)
-            for g in range(groups):
+            for g in (0, groups - 1):
                 add_halo(g, z_recv, add_dz, (side,))
 
     def plane(p, carry, inner=True):
@@ -419,6 +424,12 @@
     plane(cx - 1, 0, False)
     for s in range(2):
         start(second, 0, s, has)
+    for side in range(2):
+        @pl.when(has[2][side])
+        def _():
+            for g in range(1, groups - 1):
+                add_halo(g, z_recv, add_dz, (side,))
+
     lax.fori_loop(1, cx - 1, plane, 0)
     for s in range(2):
         start(second, 1, s, has)
@@ -461,24 +472,36 @@
     onut[:, cy - 1, :] += y_halo[1, 3]
     for d in range(3):
         sent(first, d)
+        sent(second, d)
+    sent(middle, 2)
     sent(late, 0)
     sent(plain, 0)
-    for side in range(2):
-        arrive(second, 0, side)
-    finish(0, 0)
-    finish(cx - 1, 0)
-    for side in range(2):
-        @pl.when(has[2][side])
-        def _():
-            arrive(middle, 2, side)
-            arrive(second, 2, side)
-            z_flux(side)
-
-    for g in range(groups):
-        add_halo(g, w_recv, add_res, (0, 1))
-    sent(middle, 2)
-    for d in range(3):
-        sent(second, d)
+    def end_x():
+        for side in range(2):
+            arrive(second, 0, side)
+        finish(0, 0)
+        finish(cx - 1, 0)
+
+    def end_z():
+        for side in range(2):
+            @pl.when(has[2][side])
+            def _():
+                arrive(middle, 2, side)
+                arrive(second, 2, side)
+                z_flux(side)
+
+        for g in range(groups):
+            add_halo(g, w_recv, add_res, (0, 1))
+
+    @pl.when(first_of_run)
+    def _():
+        end_z()
+        end_x()
+
+    @pl.when(not_(first_of_run))
+    def _():
+        end_x()
+        end_z()
 
 
 def out_kernel(vel_in, nut_in, vel_out, nut_out, sem):

time: 22.2 us -> 21.8 us (0.982)
  Pallas kernels: 21.4 us -> 21 us
    pallas_call x1, Pallas kernels: 20.5 us -> 20.1 us  [shards(): pl.pallas_call(functools.partial(section_kernel, counts), out_shape=(jax....]
where the time goes in v5:
time: 21.8 us; the launch traced here: 21.7 us
  Pallas kernels  21 us (96%)
  between operations  0.64 us (3%)
    pallas_call x1, Pallas kernels, shards(): pl.pallas_call(functools.partial(section_kernel, counts), out_shape=(jax....  20.1 us
    pallas_call x1, Pallas kernels, shards(): pl.pallas_call(out_kernel, out_shape=(jax.ShapeDtypeStruct(velocity.shape...  0.98 us

profile of v5, /device:TPU:6, one launch (start us, length us, event | category | flops | bytes accessed | tf_op | source)
XLA Modules:
  0.0 21.7 jit_solution(2596887838429989334)
XLA Ops:
  0.6 20.1 %section_adjoint.1 = (f32[3,16,32,128]{3,2,1,0:T(8,128)S(1)}, f32[16,32,128]{2,1,0:T(8,128)S(1)}) custom-call(f32[3,16,32,128]{3,2,1,0:T(8,128)} %vel.1, f32[16,32,128]{2,1,0:T(8,128)} %nut.1, f32[3,16,32,128]{3,2,1,0:T(8,128)} %bvel.1, f32[16,32,128]{2,1,0:T(8,128)} %bnut.1, s32[16,32,128]{2,1,0:T(8,128)} %bins.1, s32[16,32,128]{2,1,0:T(8,128)} %mask.1, f32[32]{0:T(128)} %dist.1), custom_call_target="tpu_custom_call" | custom-call | tf_op jit(solution)/shard_map/section_adjoint/pallas_call | solution.py:526
  20.7 1.0 %section_result.1 = (f32[3,16,32,128]{3,2,1,0:T(8,128)}, f32[16,32,128]{2,1,0:T(8,128)}) custom-call(f32[3,16,32,128]{3,2,1,0:T(8,128)S(1)} %get-tuple-element.4.vel_in, f32[16,32,128]{2,1,0:T(8,128)S(1)} %get-tuple-element.5.nut_in), custom_call_target="tpu_custom_call" | custom-call | tf_op jit(solution)/shard_map/section_result/pallas_call | solution.py:566

commit v6 on v5

--- a/solution.py
+++ b/solution.py
@@ -256,7 +256,7 @@
             set_parts(f, p, q[f, p + 1, rows, :])
         return carry
 
-    lax.fori_loop(0, cx, part_plane, 0)
+    lax.fori_loop(0, cx, part_plane, 0, unroll=4)
     for g in range(groups):
         along_z(g, None, z_send, (0, 1))
 
@@ -301,7 +301,7 @@
             near[p, here, :] = jnp.take_along_axis(table, bin_v[p, here, :], axis=1)
         return carry
 
-    lax.fori_loop(0, cx, look, 0)
+    lax.fori_loop(0, cx, look, 0, unroll=4)
 
     def extract(value, count, dst, base=0):
         def body(p, carry):
@@ -309,7 +309,7 @@
                 set_parts(f, p, value(f, p))
             return carry
 
-        lax.fori_loop(0, cx, body, 0)
+        lax.fori_loop(0, cx, body, 0, unroll=4)
         for g in range(groups):
             along_z(g, None, dst, (0, 1), count, base)
 
@@ -456,7 +456,7 @@
                     onut[p, here, :] += value
         return carry
 
-    lax.fori_loop(1, cx - 1, finish, 0)
+    lax.fori_loop(1, cx - 1, finish, 0, unroll=2)
     for side in range(2):
         arrive(late, 0, side)
         arrive(plain, 0, side)

time: 21.8 us -> 21.6 us (level)
    pallas_call x1, Pallas kernels: 20.1 us -> 19.8 us  [shards(): pl.pallas_call(functools.partial(section_kernel, counts), out_shape=(jax....]
where the time goes in v6:
time: 21.6 us; the launch traced here: 21.4 us
  Pallas kernels  20.8 us (96%)
  between operations  0.64 us (3%)
    pallas_call x1, Pallas kernels, shards(): pl.pallas_call(functools.partial(section_kernel, counts), out_shape=(jax....  19.8 us
    pallas_call x1, Pallas kernels, shards(): pl.pallas_call(out_kernel, out_shape=(jax.ShapeDtypeStruct(velocity.shape...  0.98 us

profile of v6, /device:TPU:6, one launch (start us, length us, event | category | flops | bytes accessed | tf_op | source)
XLA Modules:
  0.0 21.4 jit_solution(2997962661947825741)
XLA Ops:
  0.6 19.8 %section_adjoint.1 = (f32[3,16,32,128]{3,2,1,0:T(8,128)S(1)}, f32[16,32,128]{2,1,0:T(8,128)S(1)}) custom-call(f32[3,16,32,128]{3,2,1,0:T(8,128)} %vel.1, f32[16,32,128]{2,1,0:T(8,128)} %nut.1, f32[3,16,32,128]{3,2,1,0:T(8,128)} %bvel.1, f32[16,32,128]{2,1,0:T(8,128)} %bnut.1, s32[16,32,128]{2,1,0:T(8,128)} %bins.1, s32[16,32,128]{2,1,0:T(8,128)} %mask.1, f32[32]{0:T(128)} %dist.1), custom_call_target="tpu_custom_call" | custom-call | tf_op jit(solution)/shard_map/section_adjoint/pallas_call | solution.py:526
  20.5 1.0 %section_result.1 = (f32[3,16,32,128]{3,2,1,0:T(8,128)}, f32[16,32,128]{2,1,0:T(8,128)}) custom-call(f32[3,16,32,128]{3,2,1,0:T(8,128)S(1)} %get-tuple-element.4.vel_in, f32[16,32,128]{2,1,0:T(8,128)S(1)} %get-tuple-element.5.nut_in), custom_call_target="tpu_custom_call" | custom-call | tf_op jit(solution)/shard_map/section_result/pallas_call | solution.py:566

commit v7 on v6

--- a/solution.py
+++ b/solution.py
@@ -520,7 +520,7 @@
     cx, cy, cz = nut_field.shape
     f32 = jnp.float32
     group = LANES // cy
-    packed = (2, 4 * (cx // group), LANES)
+    packed = (3, 4 * (cx // group), LANES)
     hbm = pl.BlockSpec(memory_space=pltpu.HBM)
     vmem = pl.BlockSpec(memory_space=pltpu.VMEM)
     result = pl.pallas_call(
@@ -549,8 +549,8 @@
             pltpu.VMEM(packed, f32),
             pltpu.VMEM(packed, f32),
             pltpu.VMEM(packed, f32),
-            pltpu.VMEM((2, 2 * packed[1], LANES), f32),
-            pltpu.VMEM((2, 2 * packed[1], LANES), f32),
+            pltpu.VMEM((3, 2 * packed[1], LANES), f32),
+            pltpu.VMEM((3, 2 * packed[1], LANES), f32),
             pltpu.VMEM(packed, f32),
             pltpu.VMEM(packed, f32),
             pltpu.SemaphoreType.DMA((7,)),

time: 21.6 us -> 21.6 us (level)
  no operation moved by 1% of the time
where the time goes in v7:
time: 21.6 us; the launch traced here: 21.4 us
  Pallas kernels  20.8 us (96%)
  between operations  0.64 us (3%)
    pallas_call x1, Pallas kernels, shards(): pl.pallas_call(functools.partial(section_kernel, counts), out_shape=(jax....  19.8 us
    pallas_call x1, Pallas kernels, shards(): pl.pallas_call(out_kernel, out_shape=(jax.ShapeDtypeStruct(velocity.shape...  0.98 us

profile of v7, /device:TPU:6, one launch (start us, length us, event | category | flops | bytes accessed | tf_op | source)
XLA Modules:
  0.0 21.4 jit_solution(7357764467329163521)
XLA Ops:
  0.6 19.8 %section_adjoint.1 = (f32[3,16,32,128]{3,2,1,0:T(8,128)S(1)}, f32[16,32,128]{2,1,0:T(8,128)S(1)}) custom-call(f32[3,16,32,128]{3,2,1,0:T(8,128)} %vel.1, f32[16,32,128]{2,1,0:T(8,128)} %nut.1, f32[3,16,32,128]{3,2,1,0:T(8,128)} %bvel.1, f32[16,32,128]{2,1,0:T(8,128)} %bnut.1, s32[16,32,128]{2,1,0:T(8,128)} %bins.1, s32[16,32,128]{2,1,0:T(8,128)} %mask.1, f32[32]{0:T(128)} %dist.1), custom_call_target="tpu_custom_call" | custom-call | tf_op jit(solution)/shard_map/section_adjoint/pallas_call | solution.py:526
  20.5 1.0 %section_result.1 = (f32[3,16,32,128]{3,2,1,0:T(8,128)}, f32[16,32,128]{2,1,0:T(8,128)}) custom-call(f32[3,16,32,128]{3,2,1,0:T(8,128)S(1)} %get-tuple-element.4.vel_in, f32[16,32,128]{2,1,0:T(8,128)S(1)} %get-tuple-element.5.nut_in), custom_call_target="tpu_custom_call" | custom-call | tf_op jit(solution)/shard_map/section_result/pallas_call | solution.py:566
